TPU v7x, 256 devices: a whole 4x4x8 slice. The times are simulated.
256 devices in a mesh: ctx: 128 (over y_lo, x, z, core), dp: 2 (over y_hi).
Axes of the slice: x: 4, y: 4 (y_hi: 2, y_lo: 2; y = y_hi * 2 + y_lo), z: 8, core: 2. Of those that a mesh axis runs over, the one named last changes fastest.
Arguments:
- queries: bfloat16 [32768, 1024], P(('dp', 'ctx')), parts along dimension 0, may hold values from -6 to 6
- keys: bfloat16 [32768, 1024], P(('dp', 'ctx')), parts along dimension 0, may hold values from -6 to 6
- values: bfloat16 [32768, 1024], P(('dp', 'ctx')), parts along dimension 0, may hold values from -6 to 6
- cotangent: bfloat16 [32768, 1024], P(('dp', 'ctx')), parts along dimension 0, may hold values from -6 to 6
- doc_lengths: int32 [128], P('dp'), parts along dimension 0, may hold values from 1 to 512, 16384 in all
Outputs:
- attended: bfloat16 [32768, 1024], P(('dp', 'ctx')), parts along dimension 0
- query_grad: bfloat16 [32768, 1024], P(('dp', 'ctx')), parts along dimension 0
- key_grad: bfloat16 [32768, 1024], P(('dp', 'ctx')), parts along dimension 0
- value_grad: bfloat16 [32768, 1024], P(('dp', 'ctx')), parts along dimension 0
There are 2 independent parts, one for each index of `dp`. A program takes and returns all parts, laid end to end along the dimension named above; each array names one. Nothing has to cross between parts.
Inputs may be any that keep to these rules, and one draw needn't show every extreme that they name: `doc_lengths`: the 64 lengths sum to 16384; the longest is exactly 512.
All inputs are finite; a program needn't handle non-finite values.
Results may differ from a plain program's by a relative error of at most 0.027.
Values may be sent and summed in bfloat16 or wider, within the bound.
A program may use at most 64 MiB of HBM per device.

v0:
```python
import jax
import jax.numpy as jnp
from jax import lax
from jax.sharding import PartitionSpec as P

H = 16
DH = 64
REACH = 4


def from_behind(block, axis, distance):
    devices = range(lax.axis_size(axis))
    route = [(i - distance, i) for i in devices if i - distance in devices]
    return lax.ppermute(block, axis, route)


def segment_ids(doc_ends, start, count, total_tokens):
    position = start + jnp.arange(count, dtype=jnp.int32)
    found = jnp.sum((doc_ends[None, :] <= position[:, None]).astype(jnp.int32), axis=1)
    inside = (position >= 0) & (position < total_tokens)
    return jnp.where(inside, found, -1)


def shares_document(query_ids, key_ids):
    key_high = jnp.max(key_ids)
    key_low = jnp.min(jnp.where(key_ids >= 0, key_ids, 1 << 30))
    return (key_high >= jnp.min(query_ids)) & (key_low <= jnp.max(query_ids))


def on_device(queries, keys, values, cotangent, doc_lengths):
    row_count, feature_count = queries.shape
    head_count = H
    head_size = DH
    score_scale = float(head_size) ** (-0.5)
    position = lax.axis_index("ctx")
    members = lax.axis_size("ctx")
    total_tokens = row_count * members
    doc_ends = jnp.cumsum(doc_lengths)
    query_ids = segment_ids(doc_ends, position * row_count, row_count, total_tokens)
    packed = jnp.stack([keys, values])
    blocks = {0: packed}
    from_above = packed
    from_below = packed
    for distance in range(1, REACH + 1):
        from_above = from_behind(from_above, "ctx", -1)
        blocks[distance] = from_above
    for distance in range(1, REACH + 1):
        from_below = from_behind(from_below, "ctx", 1)
        blocks[-distance] = from_below
    offsets = [0] + list(range(1, REACH + 1)) + [-d for d in range(1, REACH + 1)]
    key_ids = {}
    shared = {}
    for offset in offsets:
        key_ids[offset] = segment_ids(
            doc_ends, (position + offset) * row_count, row_count, total_tokens
        )
        shared[offset] = shares_document(query_ids, key_ids[offset])
    query_heads = queries.reshape(row_count, head_count, head_size)
    cotangent_heads = cotangent.reshape(row_count, head_count, head_size)

    def scores_of(offset):
        key_heads = blocks[offset][0].reshape(row_count, head_count, head_size)
        scores = (
            jnp.einsum("qhd,khd->hqk", query_heads, key_heads, preferred_element_type=jnp.float32)
            * score_scale
        )
        same = query_ids[:, None] == key_ids[offset][None, :]
        return jnp.where(same[None], scores, -jnp.inf)

    row_max = jnp.full((head_count, row_count), -jnp.inf, jnp.float32)
    row_sum = jnp.zeros((head_count, row_count), jnp.float32)
    for offset in offsets:

        def update(state, offset=offset):
            scores = scores_of(offset)
            new_max = jnp.maximum(state[0], jnp.max(scores, axis=2))
            new_sum = state[1] * jnp.exp(state[0] - new_max) + jnp.sum(
                jnp.exp(scores - new_max[:, :, None]), axis=2
            )
            return (new_max, new_sum)

        row_max, row_sum = update((row_max, row_sum))
    lse = row_max + jnp.log(row_sum)
    output = jnp.zeros((row_count, head_count, head_size), jnp.float32)
    for offset in offsets:

        def add_out(state, offset=offset):
            value_heads = blocks[offset][1].reshape(row_count, head_count, head_size)
            probs_low = jnp.exp(scores_of(offset) - lse[:, :, None]).astype(jnp.bfloat16)
            return state + jnp.einsum(
                "hqk,khd->qhd", probs_low, value_heads, preferred_element_type=jnp.float32
            )

        output = add_out(output)
    attended_heads = output.astype(jnp.bfloat16)
    row_delta = jnp.sum(
        cotangent_heads.astype(jnp.float32) * attended_heads.astype(jnp.float32), axis=2
    ).T
    query_total = jnp.zeros((row_count, head_count, head_size), jnp.float32)
    grads = {}
    for offset in offsets:

        def backward(state, offset=offset):
            key_heads = blocks[offset][0].reshape(row_count, head_count, head_size)
            value_heads = blocks[offset][1].reshape(row_count, head_count, head_size)
            probs = jnp.exp(scores_of(offset) - lse[:, :, None])
            probs_low = probs.astype(jnp.bfloat16)
            prob_grads = jnp.einsum(
                "qhd,khd->hqk", cotangent_heads, value_heads, preferred_element_type=jnp.float32
            )
            score_grads = (probs * (prob_grads - row_delta[:, :, None])).astype(jnp.bfloat16)
            query_part = jnp.einsum(
                "hqk,khd->qhd", score_grads, key_heads, preferred_element_type=jnp.float32
            )
            key_part = (
                jnp.einsum(
                    "hqk,qhd->khd", score_grads, query_heads, preferred_element_type=jnp.float32
                )
                * score_scale
            )
            value_part = jnp.einsum(
                "hqk,qhd->khd", probs_low, cotangent_heads, preferred_element_type=jnp.float32
            )
            pieces = jnp.stack(
                [
                    key_part.reshape(row_count, feature_count),
                    value_part.reshape(row_count, feature_count),
                ]
            )
            return (state + query_part, pieces)

        query_total, grads[offset] = backward(query_total)
    rounded = {}
    for offset in offsets:
        if offset != 0:
            rounded[offset] = grads[offset].astype(jnp.bfloat16)
    upward_terms = rounded[REACH][None]
    for distance in range(REACH - 1, -1, -1):
        upward_terms = from_behind(upward_terms, "ctx", 1)
        if distance > 0:
            upward_terms = jnp.concatenate([upward_terms, rounded[distance][None]], axis=0)
    downward_terms = rounded[-REACH][None]
    for distance in range(REACH - 1, -1, -1):
        downward_terms = from_behind(downward_terms, "ctx", -1)
        if distance > 0:
            downward_terms = jnp.concatenate([downward_terms, rounded[-distance][None]], axis=0)
    upward = jnp.sum(upward_terms.astype(jnp.float32), axis=0)
    downward = jnp.sum(downward_terms.astype(jnp.float32), axis=0)
    owned = grads[0] + upward + downward
    attended = attended_heads.reshape(row_count, feature_count)
    query_grad = (query_total * score_scale).astype(jnp.bfloat16).reshape(row_count, feature_count)
    key_grad = owned[0].astype(jnp.bfloat16)
    value_grad = owned[1].astype(jnp.bfloat16)
    return (attended, query_grad, key_grad, value_grad)


def solution(mesh):
    placed = (
        P(("dp", "ctx"), None),
        P(("dp", "ctx"), None),
        P(("dp", "ctx"), None),
        P(("dp", "ctx"), None),
        P("dp"),
    )
    return jax.shard_map(
        on_device,
        mesh=mesh,
        in_specs=placed,
        out_specs=(
            P(("dp", "ctx"), None),
            P(("dp", "ctx"), None),
            P(("dp", "ctx"), None),
            P(("dp", "ctx"), None),
        ),
        check_vma=False,
    )
```

profile of v0, /device:TPU:24, one launch (start us, length us, event | category | flops | bytes accessed | tf_op | source)
XLA Modules:
  0.0 228.1 jit_solution(11120616272842613928)
XLA Ops:
  1.8 9.6 %collective-permute-start = (bf16[2,128,1024]{2,1,0:T(8,128)(2,1)S(1)}, bf16[2,128,1024]{2,1,0:T(8,128)(2,1)}, u32[]{:S(2)}, u32[]{:S(2)}) collective-permute-start(bf16[2,128,1024]{2,1,0:T(8,128)(2,1)S(1)} %pad_maximum_fusion), channel_id=1, source_target_pairs={{2,0},{4,2},{6,4},{8,6},{10,8},{12,10},{14,12},{16,14},{18,16},{20... | collective-permute-start | bytes 1572872 | tf_op jit(solution)/shard_map/ppermute | solution.py:14
  11.4 1.9 collective-permute-start.4
  18.3 7.9 %collective-permute-done.4 = bf16[2,128,1024]{2,1,0:T(8,128)(2,1)} collective-permute-done((bf16[2,128,1024]{2,1,0:T(8,128)(2,1)S(1)}, bf16[2,128,1024]{2,1,0:T(8,128)(2,1)}, u32[]{:S(2)}, u32[]{:S(2)}) %collective-permute-start.4) | collective-permute-done | bytes 524320 | tf_op jit(solution)/shard_map/ppermute | solution.py:14
  26.2 1.8 fusion.105
  28.2 1.9 fusion.104
  30.2 1.9 collective-permute-start.1
  32.1 2.4 %collective-permute-start.5 = (bf16[2,128,1024]{2,1,0:T(8,128)(2,1)}, bf16[2,128,1024]{2,1,0:T(8,128)(2,1)}, u32[]{:S(2)}, u32[]{:S(2)}) collective-permute-start(bf16[2,128,1024]{2,1,0:T(8,128)(2,1)} %collective-permute-done.4), channel_id=1, source_target_pairs={{0,2},{2,4},{4,6},{6,8},{8,10},{10,12},{12,14},{14,16},{16,18},{18... | collective-permute-start | bytes 1572872 | tf_op jit(solution)/shard_map/ppermute | solution.py:14
  36.3 1.8 copy.231
  38.1 1.8 copy.239
  39.9 7.2 %collective-permute-done.5 = bf16[2,128,1024]{2,1,0:T(8,128)(2,1)} collective-permute-done((bf16[2,128,1024]{2,1,0:T(8,128)(2,1)}, bf16[2,128,1024]{2,1,0:T(8,128)(2,1)}, u32[]{:S(2)}, u32[]{:S(2)}) %collective-permute-start.5) | collective-permute-done | bytes 524320 | tf_op jit(solution)/shard_map/ppermute | solution.py:14
  47.2 1.9 fusion.106
  50.2 1.9 collective-permute-start.6
  53.5 7.8 %collective-permute-start.2 = (bf16[2,128,1024]{2,1,0:T(8,128)(2,1)}, bf16[2,128,1024]{2,1,0:T(8,128)(2,1)}, u32[]{:S(2)}, u32[]{:S(2)}) collective-permute-start(bf16[2,128,1024]{2,1,0:T(8,128)(2,1)} %collective-permute-done.1), channel_id=1, source_target_pairs={{2,0},{4,2},{6,4},{8,6},{10,8},{12,10},{14,12},{16,14},{18,16},{20... | collective-permute-start | bytes 1572872 | tf_op jit(solution)/shard_map/ppermute | solution.py:14
  61.3 1.9 fusion.103
  64.3 1.9 copy.233
  66.2 1.8 copy.241
  69.3 1.9 fusion.107
  71.2 1.8 copy.227
  73.0 3.4 %collective-permute-start.3 = (bf16[2,128,1024]{2,1,0:T(8,128)(2,1)}, bf16[2,128,1024]{2,1,0:T(8,128)(2,1)}, u32[]{:S(2)}, u32[]{:S(2)}) collective-permute-start(bf16[2,128,1024]{2,1,0:T(8,128)(2,1)} %collective-permute-done.2), channel_id=1, source_target_pairs={{2,0},{4,2},{6,4},{8,6},{10,8},{12,10},{14,12},{16,14},{18,16},{20... | collective-permute-start | bytes 1572872 | tf_op jit(solution)/shard_map/ppermute | solution.py:14
  76.3 2.3 %fusion.110 = (f32[16,128]{1,0:T(8,128)S(1)}, f32[16,128,128]{1,2,0:T(8,128)}) fusion(bf16[128,16,64]{0,2,1:T(8,128)(2,1)} %bitcast.379, bf16[128,16,64]{0,2,1:T(8,128)(2,1)S(1)} %bitcast.352, pred[128,128]{0,1:T(8,128)(4,1)S(1)} %get-tuple-element.61), kind=kOutput, calls=%fused_computation.215 | convolution fusion | flops 34338816 | bytes 1597440 | tf_op jit(solution)/shard_map/qhd,khd->hqk/dot_general | solution.py:64
  78.6 2.1 collective-permute-start.7
  80.7 1.9 fusion.102
  83.7 1.9 copy.235
  85.6 1.8 copy.243
  88.8 1.9 fusion.101
  91.7 1.9 collective-permute-done.7
  93.7 1.9 fusion.108
  95.5 1.8 copy.228
  97.7 1.9 fusion.109
  106.4 1.8 copy.245
  108.2 2.4 %convolution_bitcast_fusion.10 = f32[128,16,64]{0,2,1:T(8,128)} fusion(bf16[128,16,64]{0,2,1:T(8,128)(2,1)} %bitcast.397, f32[16,128,128]{1,2,0:T(8,128)} %copy-done.10, f32[16,128]{1,0:T(8,128)S(1)} %log_add_fusion), kind=kOutput, calls=%fused_computation.77 | convolution fusion | flops 34078720 | bytes 1843200 | tf_op jit(solution)/shard_map/hqk,khd->qhd/dot_general | solution.py:90
  110.6 1.8 copy.237
  112.4 1.8 convolution_convert_fusion.7
  125.5 1.9 collective-permute-start.8
  127.5 7.9 %collective-permute-start.12 = (bf16[1,2,128,1024]{2,3,1,0:T(8,128)(2,1)S(1)}, bf16[1,2,128,1024]{2,3,1,0:T(8,128)(2,1)S(1)}, u32[]{:S(2)}, u32[]{:S(2)}) collective-permute-start(bf16[1,2,128,1024]{2,3,1,0:T(8,128)(2,1)S(1)} %pad_maximum_fusion.2), channel_id=1, source_target_pairs={{2,0},{4,2},{6,4},{8,6},{10,8},{12,10},{14,12},{16,14},{18,16},{20... | collective-permute-start | bytes 1572872 | tf_op jit(solution)/shard_map/ppermute | solution.py:14
  136.8 3.4 %collective-permute-done.8 = bf16[1,2,128,1024]{2,3,1,0:T(8,128)(2,1)S(1)} collective-permute-done((bf16[1,2,128,1024]{2,3,1,0:T(8,128)(2,1)S(1)}, bf16[1,2,128,1024]{2,3,1,0:T(8,128)(2,1)S(1)}, u32[]{:S(2)}, u32[]{:S(2)}) %collective-permute-start.8) | collective-permute-done | bytes 524320 | tf_op jit(solution)/shard_map/ppermute | solution.py:14
  140.4 2.3 collective-permute-start.9
  143.2 8.0 %collective-permute-start.13 = (bf16[2,2,128,1024]{2,3,1,0:T(8,128)(2,1)S(1)}, bf16[2,2,128,1024]{2,3,1,0:T(8,128)(2,1)S(1)}, u32[]{:S(2)}, u32[]{:S(2)}) collective-permute-start(bf16[2,2,128,1024]{2,3,1,0:T(8,128)(2,1)S(1)} %maximum_maximum_fusion.5), channel_id=1, source_target_pairs={{2,0},{4,2},{6,4},{8,6},{10,8},{12,10},{14,12},{16,14},{18,16},{20... | collective-permute-start | bytes 3145736 | tf_op jit(solution)/shard_map/ppermute | solution.py:14
  152.5 8.3 %collective-permute-done.9 = bf16[2,2,128,1024]{2,3,1,0:T(8,128)(2,1)S(1)} collective-permute-done((bf16[2,2,128,1024]{2,3,1,0:T(8,128)(2,1)S(1)}, bf16[2,2,128,1024]{2,3,1,0:T(8,128)(2,1)S(1)}, u32[]{:S(2)}, u32[]{:S(2)}) %collective-permute-start.9) | collective-permute-done | bytes 1048608 | tf_op jit(solution)/shard_map/ppermute | solution.py:14
  161.0 1.9 collective-permute-start.10
  163.7 8.0 %collective-permute-start.14 = (bf16[3,2,128,1024]{2,3,1,0:T(8,128)(2,1)S(1)}, bf16[3,2,128,1024]{2,3,1,0:T(8,128)(2,1)S(1)}, u32[]{:S(2)}, u32[]{:S(2)}) collective-permute-start(bf16[3,2,128,1024]{2,3,1,0:T(8,128)(2,1)S(1)} %maximum_maximum_fusion.3), channel_id=1, source_target_pairs={{2,0},{4,2},{6,4},{8,6},{10,8},{12,10},{14,12},{16,14},{18,16},{20... | collective-permute-start | bytes 4718600 | tf_op jit(solution)/shard_map/ppermute | solution.py:14
  173.8 13.1 %collective-permute-done.10 = bf16[3,2,128,1024]{2,3,1,0:T(8,128)(2,1)S(1)} collective-permute-done((bf16[3,2,128,1024]{2,3,1,0:T(8,128)(2,1)S(1)}, bf16[3,2,128,1024]{2,3,1,0:T(8,128)(2,1)S(1)}, u32[]{:S(2)}, u32[]{:S(2)}) %collective-permute-start.10) | collective-permute-done | bytes 1572896 | tf_op jit(solution)/shard_map/ppermute | solution.py:14
  188.4 1.9 collective-permute-start.11
  192.3 8.0 %collective-permute-start.15 = (bf16[4,2,128,1024]{2,3,1,0:T(8,128)(2,1)}, bf16[4,2,128,1024]{2,3,1,0:T(8,128)(2,1)}, u32[]{:S(2)}, u32[]{:S(2)}) collective-permute-start(bf16[4,2,128,1024]{2,3,1,0:T(8,128)(2,1)} %maximum_maximum_fusion.1), channel_id=1, source_target_pairs={{2,0},{4,2},{6,4},{8,6},{10,8},{12,10},{14,12},{16,14},{18,16},{20... | collective-permute-start | bytes 6291464 | tf_op jit(solution)/shard_map/ppermute | solution.py:14
  204.8 15.5 %collective-permute-done.11 = bf16[4,2,128,1024]{2,3,1,0:T(8,128)(2,1)} collective-permute-done((bf16[4,2,128,1024]{2,3,1,0:T(8,128)(2,1)}, bf16[4,2,128,1024]{2,3,1,0:T(8,128)(2,1)}, u32[]{:S(2)}, u32[]{:S(2)}) %collective-permute-start.11) | collective-permute-done | bytes 2097184 | tf_op jit(solution)/shard_map/ppermute | solution.py:14
  220.3 2.0 convert_reduce_fusion.1
  222.3 1.9 collective-permute-done.15
  224.2 2.0 convert_reduce_fusion
  (205 shorter events, 50.9 us)
Async XLA Ops:
  0.6 15.9 %copy-start.42 = (bf16[128,1024]{1,0:T(8,128)(2,1)S(1)}, bf16[128,1024]{1,0:T(8,128)(2,1)}, u32[]{:S(2)}) copy-start(bf16[128,1024]{1,0:T(8,128)(2,1)} %param.7) | copy-start | bytes 786436
  0.6 15.3 %copy-start.43 = (bf16[128,1024]{1,0:T(8,128)(2,1)S(1)}, bf16[128,1024]{1,0:T(8,128)(2,1)}, u32[]{:S(2)}) copy-start(bf16[128,1024]{1,0:T(8,128)(2,1)} %param.5) | copy-start | bytes 786436
  0.7 16.8 %copy-start.44 = (bf16[128,1024]{1,0:T(8,128)(2,1)S(1)}, bf16[128,1024]{1,0:T(8,128)(2,1)}, u32[]{:S(2)}) copy-start(bf16[128,1024]{1,0:T(8,128)(2,1)} %param.8) | copy-start | bytes 786436
  1.8 26.4 %collective-permute-start = (bf16[2,128,1024]{2,1,0:T(8,128)(2,1)S(1)}, bf16[2,128,1024]{2,1,0:T(8,128)(2,1)}, u32[]{:S(2)}, u32[]{:S(2)}) collective-permute-start(bf16[2,128,1024]{2,1,0:T(8,128)(2,1)S(1)} %pad_maximum_fusion), channel_id=1, source_target_pairs={{2,0},{4,2},{6,4},{8,6},{10,8},{12,10},{14,12},{16,14},{18,16},{20... | collective-permute-start | bytes 1572872 | tf_op jit(solution)/shard_map/ppermute | solution.py:14
  11.4 14.8 %collective-permute-start.4 = (bf16[2,128,1024]{2,1,0:T(8,128)(2,1)S(1)}, bf16[2,128,1024]{2,1,0:T(8,128)(2,1)}, u32[]{:S(2)}, u32[]{:S(2)}) collective-permute-start(bf16[2,128,1024]{2,1,0:T(8,128)(2,1)S(1)} %pad_maximum_fusion), channel_id=1, source_target_pairs={{0,2},{2,4},{4,6},{6,8},{8,10},{10,12},{12,14},{14,16},{16,18},{18... | collective-permute-start | bytes 1572872 | tf_op jit(solution)/shard_map/ppermute | solution.py:14
  28.2 8.2 %copy-start.14 = (bf16[1,128,1024]{1,2,0:T(8,128)(2,1)}, bf16[1,128,1024]{1,2,0:T(8,128)(2,1)S(1)}, u32[]{:S(2)}) copy-start(bf16[1,128,1024]{1,2,0:T(8,128)(2,1)S(1)} %copy.225) | copy-start | bytes 786436
  30.2 23.2 %collective-permute-start.1 = (bf16[2,128,1024]{2,1,0:T(8,128)(2,1)}, bf16[2,128,1024]{2,1,0:T(8,128)(2,1)}, u32[]{:S(2)}, u32[]{:S(2)}) collective-permute-start(bf16[2,128,1024]{2,1,0:T(8,128)(2,1)} %collective-permute-done), channel_id=1, source_target_pairs={{2,0},{4,2},{6,4},{8,6},{10,8},{12,10},{14,12},{16,14},{18,16},{20... | collective-permute-start | bytes 1572872 | tf_op jit(solution)/shard_map/ppermute | solution.py:14
  32.1 15.0 %collective-permute-start.5 = (bf16[2,128,1024]{2,1,0:T(8,128)(2,1)}, bf16[2,128,1024]{2,1,0:T(8,128)(2,1)}, u32[]{:S(2)}, u32[]{:S(2)}) collective-permute-start(bf16[2,128,1024]{2,1,0:T(8,128)(2,1)} %collective-permute-done.4), channel_id=1, source_target_pairs={{0,2},{2,4},{4,6},{6,8},{8,10},{10,12},{12,14},{14,16},{16,18},{18... | collective-permute-start | bytes 1572872 | tf_op jit(solution)/shard_map/ppermute | solution.py:14
  50.2 13.0 %copy-start.20 = (bf16[1,128,1024]{1,2,0:T(8,128)(2,1)}, bf16[1,128,1024]{1,2,0:T(8,128)(2,1)S(1)}, u32[]{:S(2)}) copy-start(bf16[1,128,1024]{1,2,0:T(8,128)(2,1)S(1)} %copy.226) | copy-start | bytes 786436
  50.2 19.1 %collective-permute-start.6 = (bf16[2,128,1024]{2,1,0:T(8,128)(2,1)}, bf16[2,128,1024]{2,1,0:T(8,128)(2,1)}, u32[]{:S(2)}, u32[]{:S(2)}) collective-permute-start(bf16[2,128,1024]{2,1,0:T(8,128)(2,1)} %collective-permute-done.5), channel_id=1, source_target_pairs={{0,2},{2,4},{4,6},{6,8},{8,10},{10,12},{12,14},{14,16},{16,18},{18... | collective-permute-start | bytes 1572872 | tf_op jit(solution)/shard_map/ppermute | solution.py:14
  53.5 19.5 %collective-permute-start.2 = (bf16[2,128,1024]{2,1,0:T(8,128)(2,1)}, bf16[2,128,1024]{2,1,0:T(8,128)(2,1)}, u32[]{:S(2)}, u32[]{:S(2)}) collective-permute-start(bf16[2,128,1024]{2,1,0:T(8,128)(2,1)} %collective-permute-done.1), channel_id=1, source_target_pairs={{2,0},{4,2},{6,4},{8,6},{10,8},{12,10},{14,12},{16,14},{18,16},{20... | collective-permute-start | bytes 1572872 | tf_op jit(solution)/shard_map/ppermute | solution.py:14
  64.3 8.7 %copy-start.16 = (bf16[1,128,1024]{1,2,0:T(8,128)(2,1)}, bf16[1,128,1024]{1,2,0:T(8,128)(2,1)S(1)}, u32[]{:S(2)}) copy-start(bf16[1,128,1024]{1,2,0:T(8,128)(2,1)S(1)} %copy.222) | copy-start | bytes 786436
  73.0 15.8 %collective-permute-start.3 = (bf16[2,128,1024]{2,1,0:T(8,128)(2,1)}, bf16[2,128,1024]{2,1,0:T(8,128)(2,1)}, u32[]{:S(2)}, u32[]{:S(2)}) collective-permute-start(bf16[2,128,1024]{2,1,0:T(8,128)(2,1)} %collective-permute-done.2), channel_id=1, source_target_pairs={{2,0},{4,2},{6,4},{8,6},{10,8},{12,10},{14,12},{16,14},{18,16},{20... | collective-permute-start | bytes 1572872 | tf_op jit(solution)/shard_map/ppermute | solution.py:14
  78.6 15.0 %collective-permute-start.7 = (bf16[2,128,1024]{2,1,0:T(8,128)(2,1)}, bf16[2,128,1024]{2,1,0:T(8,128)(2,1)}, u32[]{:S(2)}, u32[]{:S(2)}) collective-permute-start(bf16[2,128,1024]{2,1,0:T(8,128)(2,1)} %collective-permute-done.6), channel_id=1, source_target_pairs={{0,2},{2,4},{4,6},{6,8},{8,10},{10,12},{12,14},{14,16},{16,18},{18... | collective-permute-start | bytes 1572872 | tf_op jit(solution)/shard_map/ppermute | solution.py:14
  83.7 6.9 %copy-start.18 = (bf16[1,128,1024]{1,2,0:T(8,128)(2,1)}, bf16[1,128,1024]{1,2,0:T(8,128)(2,1)S(1)}, u32[]{:S(2)}) copy-start(bf16[1,128,1024]{1,2,0:T(8,128)(2,1)S(1)} %copy.223) | copy-start | bytes 786436
  97.3 2.3 %copy-start = (f32[16,128,128]{1,2,0:T(8,128)S(1)}, f32[16,128,128]{1,2,0:T(8,128)}, u32[]{:S(2)}) copy-start(f32[16,128,128]{1,2,0:T(8,128)} %get-tuple-element.81) | copy-start | bytes 3145732
  97.3 2.5 %copy-start.2 = (f32[16,128,128]{1,2,0:T(8,128)S(1)}, f32[16,128,128]{1,2,0:T(8,128)}, u32[]{:S(2)}) copy-start(f32[16,128,128]{1,2,0:T(8,128)} %get-tuple-element.77) | copy-start | bytes 3145732
  97.7 2.5 %copy-start.12 = (f32[16,128,128]{1,2,0:T(8,128)}, f32[16,128,128]{1,2,0:T(8,128)S(1)}, u32[]{:S(2)}) copy-start(f32[16,128,128]{1,2,0:T(8,128)S(1)} %get-tuple-element.73) | copy-start | bytes 3145732
  97.7 2.3 %copy-start.8 = (f32[16,128,128]{1,2,0:T(8,128)S(1)}, f32[16,128,128]{1,2,0:T(8,128)}, u32[]{:S(2)}) copy-start(f32[16,128,128]{1,2,0:T(8,128)} %get-tuple-element.75) | copy-start | bytes 3145732
  99.6 2.1 copy-start.10
  100.0 1.5 copy-start.6
  100.3 1.5 copy-start.45
  100.4 1.6 copy-start.24
  101.4 1.7 copy-start.27
  101.9 2.3 %copy-start.30 = (bf16[1,128,1024]{1,2,0:T(8,128)(2,1)S(1)}, bf16[1,128,1024]{1,2,0:T(8,128)(2,1)}, u32[]{:S(2)}) copy-start(bf16[1,128,1024]{1,2,0:T(8,128)(2,1)} %copy.241) | copy-start | bytes 786436
  103.0 2.3 %copy-start.32 = (bf16[1,128,1024]{1,2,0:T(8,128)(2,1)S(1)}, bf16[1,128,1024]{1,2,0:T(8,128)(2,1)}, u32[]{:S(2)}) copy-start(bf16[1,128,1024]{1,2,0:T(8,128)(2,1)} %copy.243) | copy-start | bytes 786436
  112.4 1.9 copy-start.1
  112.4 3.4 %copy-start.3 = (f32[16,128,128]{1,2,0:T(8,128)S(1)}, f32[16,128,128]{1,2,0:T(8,128)}, u32[]{:S(2)}) copy-start(f32[16,128,128]{1,2,0:T(8,128)} %get-tuple-element.77) | copy-start | bytes 3145732
  112.4 3.4 %copy-start.29 = (bf16[1,128,1024]{1,2,0:T(8,128)(2,1)S(1)}, bf16[1,128,1024]{1,2,0:T(8,128)(2,1)}, u32[]{:S(2)}) copy-start(bf16[1,128,1024]{1,2,0:T(8,128)(2,1)} %copy.233) | copy-start | bytes 786436
  114.2 1.9 copy-start.9
  114.2 1.9 copy-start.34
  115.8 1.6 copy-start.38
  115.8 1.7 copy-start.39
  115.8 1.9 copy-start.40
  124.7 10.7 %copy-start.21 = (bf16[1,128,1024]{1,2,0:T(8,128)(2,1)S(1)}, bf16[1,128,1024]{1,2,0:T(8,128)(2,1)}, u32[]{:S(2)}) copy-start(bf16[1,128,1024]{1,2,0:T(8,128)(2,1)} %copy-done.20) | copy-start | bytes 786436
  125.0 10.7 %copy-start.22 = (bf16[1,128,1024]{1,2,0:T(8,128)(2,1)S(1)}, bf16[1,128,1024]{1,2,0:T(8,128)(2,1)}, u32[]{:S(2)}) copy-start(bf16[1,128,1024]{1,2,0:T(8,128)(2,1)} %copy.227) | copy-start | bytes 786436
  125.5 14.7 %collective-permute-start.8 = (bf16[1,2,128,1024]{2,3,1,0:T(8,128)(2,1)S(1)}, bf16[1,2,128,1024]{2,3,1,0:T(8,128)(2,1)S(1)}, u32[]{:S(2)}, u32[]{:S(2)}) collective-permute-start(bf16[1,2,128,1024]{2,3,1,0:T(8,128)(2,1)S(1)} %pad_maximum_fusion.1), channel_id=1, source_target_pairs={{0,2},{2,4},{4,6},{6,8},{8,10},{10,12},{12,14},{14,16},{16,18},{18... | collective-permute-start | bytes 1572872 | tf_op jit(solution)/shard_map/ppermute | solution.py:14
  127.5 15.6 %collective-permute-start.12 = (bf16[1,2,128,1024]{2,3,1,0:T(8,128)(2,1)S(1)}, bf16[1,2,128,1024]{2,3,1,0:T(8,128)(2,1)S(1)}, u32[]{:S(2)}, u32[]{:S(2)}) collective-permute-start(bf16[1,2,128,1024]{2,3,1,0:T(8,128)(2,1)S(1)} %pad_maximum_fusion.2), channel_id=1, source_target_pairs={{2,0},{4,2},{6,4},{8,6},{10,8},{12,10},{14,12},{16,14},{18,16},{20... | collective-permute-start | bytes 1572872 | tf_op jit(solution)/shard_map/ppermute | solution.py:14
  140.4 11.4 %copy-start.26 = (bf16[1,128,1024]{1,2,0:T(8,128)(2,1)S(1)}, bf16[1,128,1024]{1,2,0:T(8,128)(2,1)}, u32[]{:S(2)}) copy-start(bf16[1,128,1024]{1,2,0:T(8,128)(2,1)} %copy.231) | copy-start | bytes 786436
  140.4 20.5 %collective-permute-start.9 = (bf16[2,2,128,1024]{2,3,1,0:T(8,128)(2,1)S(1)}, bf16[2,2,128,1024]{2,3,1,0:T(8,128)(2,1)S(1)}, u32[]{:S(2)}, u32[]{:S(2)}) collective-permute-start(bf16[2,2,128,1024]{2,3,1,0:T(8,128)(2,1)S(1)} %maximum_maximum_fusion.4), channel_id=1, source_target_pairs={{0,2},{2,4},{4,6},{6,8},{8,10},{10,12},{12,14},{14,16},{16,18},{18... | collective-permute-start | bytes 3145736 | tf_op jit(solution)/shard_map/ppermute | solution.py:14
  143.2 8.9 %copy-start.28 = (bf16[1,128,1024]{1,2,0:T(8,128)(2,1)S(1)}, bf16[1,128,1024]{1,2,0:T(8,128)(2,1)}, u32[]{:S(2)}) copy-start(bf16[1,128,1024]{1,2,0:T(8,128)(2,1)} %copy.239) | copy-start | bytes 786436
  143.2 20.3 %collective-permute-start.13 = (bf16[2,2,128,1024]{2,3,1,0:T(8,128)(2,1)S(1)}, bf16[2,2,128,1024]{2,3,1,0:T(8,128)(2,1)S(1)}, u32[]{:S(2)}, u32[]{:S(2)}) collective-permute-start(bf16[2,2,128,1024]{2,3,1,0:T(8,128)(2,1)S(1)} %maximum_maximum_fusion.5), channel_id=1, source_target_pairs={{2,0},{4,2},{6,4},{8,6},{10,8},{12,10},{14,12},{16,14},{18,16},{20... | collective-permute-start | bytes 3145736 | tf_op jit(solution)/shard_map/ppermute | solution.py:14
  161.0 26.0 %collective-permute-start.10 = (bf16[3,2,128,1024]{2,3,1,0:T(8,128)(2,1)S(1)}, bf16[3,2,128,1024]{2,3,1,0:T(8,128)(2,1)S(1)}, u32[]{:S(2)}, u32[]{:S(2)}) collective-permute-start(bf16[3,2,128,1024]{2,3,1,0:T(8,128)(2,1)S(1)} %maximum_maximum_fusion.2), channel_id=1, source_target_pairs={{0,2},{2,4},{4,6},{6,8},{8,10},{10,12},{12,14},{14,16},{16,18},{18... | collective-permute-start | bytes 4718600 | tf_op jit(solution)/shard_map/ppermute | solution.py:14
  163.5 8.7 %copy-start.15 = (bf16[1,128,1024]{1,2,0:T(8,128)(2,1)S(1)}, bf16[1,128,1024]{1,2,0:T(8,128)(2,1)}, u32[]{:S(2)}) copy-start(bf16[1,128,1024]{1,2,0:T(8,128)(2,1)} %copy-done.14) | copy-start | bytes 786436
  163.7 27.1 %collective-permute-start.14 = (bf16[3,2,128,1024]{2,3,1,0:T(8,128)(2,1)S(1)}, bf16[3,2,128,1024]{2,3,1,0:T(8,128)(2,1)S(1)}, u32[]{:S(2)}, u32[]{:S(2)}) collective-permute-start(bf16[3,2,128,1024]{2,3,1,0:T(8,128)(2,1)S(1)} %maximum_maximum_fusion.3), channel_id=1, source_target_pairs={{2,0},{4,2},{6,4},{8,6},{10,8},{12,10},{14,12},{16,14},{18,16},{20... | collective-permute-start | bytes 4718600 | tf_op jit(solution)/shard_map/ppermute | solution.py:14
  188.4 31.9 %collective-permute-start.11 = (bf16[4,2,128,1024]{2,3,1,0:T(8,128)(2,1)}, bf16[4,2,128,1024]{2,3,1,0:T(8,128)(2,1)}, u32[]{:S(2)}, u32[]{:S(2)}) collective-permute-start(bf16[4,2,128,1024]{2,3,1,0:T(8,128)(2,1)} %maximum_maximum_fusion), channel_id=1, source_target_pairs={{0,2},{2,4},{4,6},{6,8},{8,10},{10,12},{12,14},{14,16},{16,18},{18... | collective-permute-start | bytes 6291464 | tf_op jit(solution)/shard_map/ppermute | solution.py:14
  192.3 8.5 %copy-start.17 = (bf16[1,128,1024]{1,2,0:T(8,128)(2,1)S(1)}, bf16[1,128,1024]{1,2,0:T(8,128)(2,1)}, u32[]{:S(2)}) copy-start(bf16[1,128,1024]{1,2,0:T(8,128)(2,1)} %copy-done.16) | copy-start | bytes 786436
  192.3 31.8 %collective-permute-start.15 = (bf16[4,2,128,1024]{2,3,1,0:T(8,128)(2,1)}, bf16[4,2,128,1024]{2,3,1,0:T(8,128)(2,1)}, u32[]{:S(2)}, u32[]{:S(2)}) collective-permute-start(bf16[4,2,128,1024]{2,3,1,0:T(8,128)(2,1)} %maximum_maximum_fusion.1), channel_id=1, source_target_pairs={{2,0},{4,2},{6,4},{8,6},{10,8},{12,10},{14,12},{16,14},{18,16},{20... | collective-permute-start | bytes 6291464 | tf_op jit(solution)/shard_map/ppermute | solution.py:14
  (14 other events, 17.5 us)
where the time goes:
time: 230 us; the launch traced here: 228 us
  starting transfers between devices  70.9 us (31%)
  waiting for transfers between devices  59.4 us (26%)
  local copies, waits for them, and re-layouts  47.8 us (21%)
  matrix products  36.5 us (16%)
  other arithmetic  11.7 us (5%)
    ppermute x16, starting transfers between devices, from_behind(): return lax.ppermute(block, axis, route)  70.9 us
    ppermute x16, waiting for transfers between devices, from_behind(): return lax.ppermute(block, axis, route)  59.4 us
    slice x15, local copies, waits for them, and re-layouts, add_out(): value_heads = blocks[offset][1].reshape(row_count, head_count, head_size)  27.4 us
    dot_general x9, matrix products, scores_of(): jnp.einsum('qhd,khd->hqk', query_heads, key_heads, preferred_element_type...  10.7 us
    slice x9, local copies, waits for them, and re-layouts, scores_of(): key_heads = blocks[offset][0].reshape(row_count, head_count, head_size)  10.2 us
    dot_general x9, matrix products, add_out(): jnp.einsum('hqk,khd->qhd', probs_low, value_heads, preferred_element_type...  10 us
    unnamed x100, local copies, waits for them, and re-layouts  9.38 us
    dot_general x9, matrix products, backward(): jnp.einsum('hqk,qhd->khd', probs_low, cotangent_heads, preferred_element_...  5.64 us
  transfers between devices with their start and end apart: 16, of which 9 were waited for; matrix products, arithmetic and copies ran while one was open for 25% of the time, Pallas kernels for 0%

commit v1 on v0

v1 whole, which is shorter than its diff:
```python
import functools

import jax
import jax.numpy as jnp
from jax import lax
from jax.experimental import pallas as pl
from jax.experimental.pallas import tpu as pltpu
from jax.sharding import PartitionSpec as P

H = 16
DH = 64
ROWS = 128
CHIP = 2 * ROWS
HEADS = H // 2
LAG = 2
SLOTS = HEADS + LAG
CHUNK = 256
LOG2E = 1.4426950408889634
F32 = jnp.float32
BF16 = jnp.bfloat16


def low_lanes(shape):
    return lax.broadcasted_iota(jnp.int32, shape, 1) < DH


def join(left, right, half):
    lanes = slice(0, DH) if half == 0 else slice(DH, 2 * DH)
    return jnp.concatenate([left[:, lanes], right[:, lanes]], axis=1)


def token_info(ends, base, axis, total):
    shape = (CHIP, 1) if axis == 0 else (1, CHIP)
    place = lax.broadcasted_iota(jnp.int32, shape, axis).astype(F32) + base
    before = ends <= place
    start = jnp.max(jnp.where(before, ends, 0.0), axis=1 - axis, keepdims=True)
    end = jnp.min(jnp.where(before, 4.0 * total, ends), axis=1 - axis, keepdims=True)
    first = jnp.floor(start * (1.0 / CHIP))
    last = jnp.floor((end - 1.0) * (1.0 / CHIP))
    owner = jnp.minimum(first + 1.0, last)
    inside = (place >= 0.0) & (place < total)
    return start, jnp.where(inside, owner, -9.0)


def kernel(
    n,
    len_ref,
    q_ref,
    k_ref,
    v_ref,
    g_ref,
    o_ref,
    dq_ref,
    dk_ref,
    dv_ref,
    own,
    stage,
    res_own,
    res_nb,
    send_r,
    send_l,
    recv_l,
    recv_r,
    fin,
    fin_out,
    fin_in,
    id_row,
    id_col,
    home,
    guest,
    sib_send,
    sib_recv,
    r_send,
    r_recv,
    l_send,
    l_recv,
    fin_send,
    fin_recv,
):
    me = lax.axis_index("ctx")
    core = lax.rem(me, 2)
    chip = lax.div(me, 2)
    sibling = me + 1 - 2 * core
    right = lax.rem(me + 2, n)
    left = lax.rem(me + n - 2, n)
    mine = pl.ds(pl.multiple_of(core * ROWS, ROWS), ROWS)
    theirs = pl.ds(pl.multiple_of((1 - core) * ROWS, ROWS), ROWS)

    barrier = pltpu.get_barrier_semaphore()
    for other in (sibling, right, left):
        pl.semaphore_signal(barrier, inc=1, device_id={"ctx": other}, device_id_type=pl.DeviceIdType.MESH)
    pl.semaphore_wait(barrier, 3)

    def remote(src, dst, send_sem, recv_sem, target):
        return pltpu.make_async_remote_copy(
            src_ref=src,
            dst_ref=dst,
            send_sem=send_sem,
            recv_sem=recv_sem,
            device_id={"ctx": target},
            device_id_type=pl.DeviceIdType.MESH,
        )

    def exchange(h):
        return remote(stage.at[h], own.at[h, :, mine], sib_send.at[h], sib_recv.at[h], sibling)

    def to_right(s, src):
        return remote(src, recv_l.at[s], r_send.at[s], r_recv.at[s], right)

    def to_left(s, src):
        return remote(src, recv_r.at[s], l_send.at[s], l_recv.at[s], left)

    def hand_back(h):
        return remote(fin_out.at[h], fin_in.at[h], fin_send.at[h], fin_recv.at[h], sibling)

    def packed(pair, half):
        lanes = pl.ds(pl.multiple_of(pair * 2 * DH, 2 * DH), 2 * DH)
        return (
            join(q_ref[:, lanes], g_ref[:, lanes], half),
            join(k_ref[:, lanes], v_ref[:, lanes], half),
        )

    def pack_theirs(pair, _):
        for half in range(2):
            h = 2 * pair + half
            a, b = packed((1 - core) * (HEADS // 2) + pair, half)
            stage[h, 0] = a
            stage[h, 1] = b
            exchange(h).start()
        return 0

    def pack_mine(pair, _):
        for half in range(2):
            h = 2 * pair + half
            a, b = packed(core * (HEADS // 2) + pair, half)
            own[h, 0, mine] = a
            own[h, 1, mine] = b
        return 0

    lax.fori_loop(0, HEADS // 2, pack_theirs, 0)
    lax.fori_loop(0, HEADS // 2, pack_mine, 0)

    for s in range(LAG):
        exchange(s).wait_recv()
        to_right(s, own.at[s]).start()
        to_left(s, own.at[s]).start()

    here = chip.astype(F32)
    total = float(n * ROWS)
    docs = len_ref.shape[1]
    across = lax.broadcasted_iota(jnp.int32, (docs, docs), 1)
    down = lax.broadcasted_iota(jnp.int32, (docs, docs), 0)
    lengths = jnp.broadcast_to(len_ref[...].astype(F32), (docs, docs))
    ends_col = jnp.sum(jnp.where(across <= down, lengths, 0.0), axis=1, keepdims=True)
    ends_row = jnp.sum(jnp.where(across == down, ends_col, 0.0), axis=0, keepdims=True)
    for axis, ends in ((1, ends_col), (0, ends_row)):
        start_o, owner_o = token_info(ends, here * CHIP, axis, total)
        start_l, owner_l = token_info(ends, (here - 1.0) * CHIP, axis, total)
        start_r, owner_r = token_info(ends, (here + 1.0) * CHIP, axis, total)
        id_own = jnp.where(owner_o == here, start_o, -1.0)
        id_nb = jnp.where(owner_l == here, start_l, jnp.where(owner_r == here, start_r, -2.0))
        if axis == 1:
            id_row[:, 0:CHIP] = id_own
            id_row[:, CHIP:] = id_nb
        else:
            id_col[0:CHIP] = jnp.broadcast_to(id_own, (CHIP, 128))
            id_col[CHIP:] = jnp.broadcast_to(id_nb, (CHIP, 128))
            home[...] = jnp.broadcast_to(owner_o - here, (CHIP, 128)).astype(BF16)
            came = jnp.where(owner_l == here, -1.0, jnp.where(owner_r == here, 1.0, 0.0))
            guest[...] = jnp.broadcast_to(came, (CHIP, 128)).astype(BF16)

    def attend(t):
        came = guest[...]
        zero = jnp.zeros((CHIP, 2 * DH), BF16)
        both = []
        for i in range(2):
            nb = jnp.where(came < 0, recv_l[t, i], jnp.where(came > 0, recv_r[t, i], zero))
            both.append(jnp.concatenate([own[t, i], nb], axis=0))
        a, b = both
        at = a.T
        bt = b.T
        none = jnp.zeros((DH, 2 * CHIP), BF16)
        qt = jnp.concatenate([at[:DH], none], axis=0)
        gt = jnp.concatenate([none, at[DH:]], axis=0)
        ids = jnp.concatenate([id_col[...]] * (CHUNK // 128), axis=1)
        low = low_lanes((2 * CHIP, 2 * DH))
        dk = jnp.zeros((2 * CHIP, 2 * DH), F32)
        dv = jnp.zeros((2 * CHIP, 2 * DH), F32)
        for c in range(2 * CHIP // CHUNK):
            part = slice(c * CHUNK, (c + 1) * CHUNK)
            scores = jnp.dot(b, qt[:, part], preferred_element_type=F32)
            scores = jnp.where(ids == id_row[:, part], scores, -jnp.inf)
            top = jnp.max(scores, axis=0, keepdims=True)
            grown = jnp.exp2((scores - top) * (LOG2E / 8.0))
            probs = grown * (1.0 / jnp.sum(grown, axis=0, keepdims=True))
            probs_low = probs.astype(BF16)
            out = jnp.dot(bt[DH:], probs_low, preferred_element_type=F32).astype(BF16).astype(F32)
            delta = jnp.sum(out * at[DH:, part].astype(F32), axis=0, keepdims=True)
            prob_grads = jnp.dot(b, gt[:, part], preferred_element_type=F32)
            score_grads = (probs * (prob_grads - delta)).astype(BF16)
            dq = jnp.dot(bt[:DH], score_grads, preferred_element_type=F32) * 0.125
            first = jnp.concatenate([dq, out], axis=0).T.astype(BF16)
            dk = dk + jnp.dot(score_grads, a[part], preferred_element_type=F32)
            dv = dv + jnp.dot(probs_low, a[part], preferred_element_type=F32)
            if c * CHUNK < CHIP:
                res_own[t, 0, part] = first
            else:
                res_nb[t, 0, c * CHUNK - CHIP : (c + 1) * CHUNK - CHIP] = first
        second = jnp.where(low, dk * 0.125, dv).astype(BF16)
        res_own[t, 1] = second[:CHIP]
        res_nb[t, 1] = second[CHIP:]

    def receive(s):
        to_right(s, own.at[0]).wait_recv()
        to_left(s, own.at[0]).wait_recv()

    def settle(s):
        h = s - LAG
        for i in range(2):
            for rows, out in ((mine, fin), (theirs, fin_out)):
                at = home[rows]
                out[h, i] = jnp.where(
                    at > 0, recv_r[s, i, rows], jnp.where(at < 0, recv_l[s, i, rows], res_own[h, i, rows])
                )
        hand_back(h).start()

    def step(t, _):
        receive(t)
        attend(t)
        s = t + LAG

        @pl.when(s < HEADS)
        def _():
            exchange(s).wait_recv()
            at = home[...]
            for i in range(2):
                send_r[t, i] = jnp.where(at > 0, own[s, i], res_nb[t, i])
                send_l[t, i] = jnp.where(at < 0, own[s, i], res_nb[t, i])
            to_right(s, send_r.at[t]).start()
            to_left(s, send_l.at[t]).start()

        @pl.when(s >= HEADS)
        def _():
            to_right(s, res_nb.at[t]).start()
            to_left(s, res_nb.at[t]).start()

        @pl.when(t >= LAG)
        def _():
            settle(t)

        return 0

    lax.fori_loop(0, HEADS, step, 0)
    for s in range(HEADS, SLOTS):
        receive(s)
        settle(s)

    def unpack(source, pair, place):
        lanes = pl.ds(pl.multiple_of(place * 2 * DH, 2 * DH), 2 * DH)
        e, o = 2 * pair, 2 * pair + 1
        dq_ref[:, lanes] = join(source[e, 0], source[o, 0], 0)
        o_ref[:, lanes] = join(source[e, 0], source[o, 0], 1)
        dk_ref[:, lanes] = join(source[e, 1], source[o, 1], 0)
        dv_ref[:, lanes] = join(source[e, 1], source[o, 1], 1)

    def unpack_mine(pair, _):
        unpack(fin, pair, core * (HEADS // 2) + pair)
        return 0

    def unpack_theirs(pair, _):
        hand_back(2 * pair).wait_recv()
        hand_back(2 * pair + 1).wait_recv()
        unpack(fin_in, pair, (1 - core) * (HEADS // 2) + pair)
        return 0

    lax.fori_loop(0, HEADS // 2, unpack_mine, 0)
    lax.fori_loop(0, HEADS // 2, unpack_theirs, 0)

    def drain(h, _):
        exchange(h).wait_send()
        hand_back(h).wait_send()
        return 0

    def drain_slots(s, _):
        to_right(s, own.at[0]).wait_send()
        to_left(s, own.at[0]).wait_send()
        return 0

    lax.fori_loop(0, HEADS, drain, 0)
    lax.fori_loop(0, SLOTS, drain_slots, 0)


def on_device(queries, keys, values, cotangent, doc_lengths):
    n = lax.axis_size("ctx")
    block = (2, CHIP, 2 * DH)
    half = (2, ROWS, 2 * DH)
    whole = pl.BlockSpec(memory_space=pltpu.VMEM)
    pairs = 2 * CHIP * 2 * CHIP * HEADS
    return pl.pallas_call(
        functools.partial(kernel, n),
        out_shape=[jax.ShapeDtypeStruct(queries.shape, BF16)] * 4,
        in_specs=[whole] * 5,
        out_specs=[whole] * 4,
        scratch_shapes=[
            pltpu.VMEM((HEADS, *block), BF16),
            pltpu.VMEM((HEADS, *half), BF16),
            pltpu.VMEM((HEADS, *block), BF16),
            pltpu.VMEM((HEADS, *block), BF16),
            pltpu.VMEM((HEADS - LAG, *block), BF16),
            pltpu.VMEM((HEADS - LAG, *block), BF16),
            pltpu.VMEM((SLOTS, *block), BF16),
            pltpu.VMEM((SLOTS, *block), BF16),
            pltpu.VMEM((HEADS, *half), BF16),
            pltpu.VMEM((HEADS, *half), BF16),
            pltpu.VMEM((HEADS, *half), BF16),
            pltpu.VMEM((1, 2 * CHIP), F32),
            pltpu.VMEM((2 * CHIP, 128), F32),
            pltpu.VMEM((CHIP, 128), BF16),
            pltpu.VMEM((CHIP, 128), BF16),
            pltpu.SemaphoreType.DMA((HEADS,)),
            pltpu.SemaphoreType.DMA((HEADS,)),
            pltpu.SemaphoreType.DMA((SLOTS,)),
            pltpu.SemaphoreType.DMA((SLOTS,)),
            pltpu.SemaphoreType.DMA((SLOTS,)),
            pltpu.SemaphoreType.DMA((SLOTS,)),
            pltpu.SemaphoreType.DMA((HEADS,)),
            pltpu.SemaphoreType.DMA((HEADS,)),
        ],
        compiler_params=pltpu.CompilerParams(
            collective_id=0, has_side_effects=True, vmem_limit_bytes=40 * 1024 * 1024
        ),
        cost_estimate=pl.CostEstimate(flops=12 * DH * pairs, bytes_accessed=1 << 21, transcendentals=pairs),
    )(doc_lengths.reshape(1, -1), queries, keys, values, cotangent)


def solution(mesh):
    rows = P(("dp", "ctx"), None)
    return jax.shard_map(
        on_device,
        mesh=mesh,
        in_specs=(rows, rows, rows, rows, P("dp")),
        out_specs=(rows, rows, rows, rows),
        check_vma=False,
    )
```

time: 230 us -> 63 us (0.27)
  the two profiles are of different devices: /device:TPU:24 before, /device:TPU:1 now
where the time goes in v1:
time: 63 us; the launch traced here: 62.8 us
  Pallas kernels  54.9 us (87%)
  local copies, waits for them, and re-layouts  7.26 us (12%)
  between operations  0.65 us (1%)
    pallas_call x1, Pallas kernels, on_device(): pl.pallas_call(functools.partial(kernel, n), out_shape=[jax.ShapeDtypeStr...  54.9 us
    unnamed x14, local copies, waits for them, and re-layouts  7.26 us

profile of v1, /device:TPU:1, one launch (start us, length us, event | category | flops | bytes accessed | tf_op | source)
XLA Modules:
  0.0 62.8 jit_solution(7416943527106370457)
XLA Ops:
  0.6 0.0 copy-start.4
  0.6 0.6 %copy-done.4 = s32[64]{0:T(128)S(1)} copy-done((s32[64]{0:T(128)S(1)}, s32[64]{0:T(128)}, u32[]{:S(2)}) %copy-start.4) | copy-done | bytes 280
  1.3 0.0 copy-start
  1.3 0.9 %copy-done = bf16[128,1024]{1,0:T(8,128)(2,1)S(1)} copy-done((bf16[128,1024]{1,0:T(8,128)(2,1)S(1)}, bf16[128,1024]{1,0:T(8,128)(2,1)}, u32[]{:S(2)}) %copy-start) | copy-done | bytes 262168
  2.2 0.0 copy-start.1
  2.2 0.9 %copy-done.1 = bf16[128,1024]{1,0:T(8,128)(2,1)S(1)} copy-done((bf16[128,1024]{1,0:T(8,128)(2,1)S(1)}, bf16[128,1024]{1,0:T(8,128)(2,1)}, u32[]{:S(2)}) %copy-start.1) | copy-done | bytes 262168
  3.2 0.0 copy-start.2
  3.2 0.9 %copy-done.2 = bf16[128,1024]{1,0:T(8,128)(2,1)S(1)} copy-done((bf16[128,1024]{1,0:T(8,128)(2,1)S(1)}, bf16[128,1024]{1,0:T(8,128)(2,1)}, u32[]{:S(2)}) %copy-start.2) | copy-done | bytes 262168
  4.1 0.0 copy-start.3
  4.1 0.9 %copy-done.3 = bf16[128,1024]{1,0:T(8,128)(2,1)S(1)} copy-done((bf16[128,1024]{1,0:T(8,128)(2,1)S(1)}, bf16[128,1024]{1,0:T(8,128)(2,1)}, u32[]{:S(2)}) %copy-start.3) | copy-done | bytes 262168
  5.1 54.9 %shard_map.84 = (bf16[128,1024]{1,0:T(8,128)(2,1)S(1)}, bf16[128,1024]{1,0:T(8,128)(2,1)S(1)}, bf16[128,1024]{1,0:T(8,128)(2,1)S(1)}, bf16[128,1024]{1,0:T(8,128)(2,1)S(1)}) custom-call(s32[1,64]{1,0:T(1,128)S(1)} %bitcast.1, bf16[128,1024]{1,0:T(8,128)(2,1)S(1)} %copy-done, bf16[128,1024]{1,0:T(8,128)(2,1)S(1)} %copy-done.1, ...), custom_call_target="tpu_custom_call" | custom-call | flops 1610612736 | bytes 2097152 | tf_op jit(solution)/shard_map/pallas_call | solution.py:299
  60.0 0.7 %copy.13 = bf16[128,1024]{1,0:T(8,128)(2,1)} copy(bf16[128,1024]{1,0:T(8,128)(2,1)S(1)} %get-tuple-element.8) | data formatting | bytes 524288
  60.7 0.7 %copy.14 = bf16[128,1024]{1,0:T(8,128)(2,1)} copy(bf16[128,1024]{1,0:T(8,128)(2,1)S(1)} %get-tuple-element.9) | data formatting | bytes 524288
  61.4 0.7 %copy.15 = bf16[128,1024]{1,0:T(8,128)(2,1)} copy(bf16[128,1024]{1,0:T(8,128)(2,1)S(1)} %get-tuple-element.10) | data formatting | bytes 524288
  62.1 0.7 %copy.16 = bf16[128,1024]{1,0:T(8,128)(2,1)} copy(bf16[128,1024]{1,0:T(8,128)(2,1)S(1)} %get-tuple-element.11) | data formatting | bytes 524288
Async XLA Ops:
  0.6 0.7 %copy-start.4 = (s32[64]{0:T(128)S(1)}, s32[64]{0:T(128)}, u32[]{:S(2)}) copy-start(s32[64]{0:T(128)} %param.9) | copy-start | bytes 772
  1.3 0.9 %copy-start = (bf16[128,1024]{1,0:T(8,128)(2,1)S(1)}, bf16[128,1024]{1,0:T(8,128)(2,1)}, u32[]{:S(2)}) copy-start(bf16[128,1024]{1,0:T(8,128)(2,1)} %q_ref.1) | copy-start | bytes 786436
  2.2 0.9 %copy-start.1 = (bf16[128,1024]{1,0:T(8,128)(2,1)S(1)}, bf16[128,1024]{1,0:T(8,128)(2,1)}, u32[]{:S(2)}) copy-start(bf16[128,1024]{1,0:T(8,128)(2,1)} %k_ref.1) | copy-start | bytes 786436
  3.2 0.9 %copy-start.2 = (bf16[128,1024]{1,0:T(8,128)(2,1)S(1)}, bf16[128,1024]{1,0:T(8,128)(2,1)}, u32[]{:S(2)}) copy-start(bf16[128,1024]{1,0:T(8,128)(2,1)} %v_ref.1) | copy-start | bytes 786436
  4.1 0.9 %copy-start.3 = (bf16[128,1024]{1,0:T(8,128)(2,1)S(1)}, bf16[128,1024]{1,0:T(8,128)(2,1)}, u32[]{:S(2)}) copy-start(bf16[128,1024]{1,0:T(8,128)(2,1)} %g_ref.1) | copy-start | bytes 786436

commit v2 on v1

v2 whole, which is shorter than its diff:
```python
import functools

import jax
import jax.numpy as jnp
from jax import lax
from jax.experimental import pallas as pl
from jax.experimental.pallas import tpu as pltpu
from jax.sharding import PartitionSpec as P

H = 16
DH = 64
ROWS = 128
CHIP = 2 * ROWS
HEADS = H // 2
LAG = 3
SLOTS = HEADS + LAG
VMEM_LIMIT = 40 * 1024 * 1024
LOG2E = 1.4426950408889634
F32 = jnp.float32
BF16 = jnp.bfloat16


def low_lanes(shape):
    return lax.broadcasted_iota(jnp.int32, shape, 1) < DH


def join(left, right, half):
    lanes = slice(0, DH) if half == 0 else slice(DH, 2 * DH)
    return jnp.concatenate([left[:, lanes], right[:, lanes]], axis=1)


def token_info(ends, base, axis, total):
    shape = (CHIP, 1) if axis == 0 else (1, CHIP)
    place = lax.broadcasted_iota(jnp.int32, shape, axis).astype(F32) + base
    before = ends <= place
    start = jnp.max(jnp.where(before, ends, 0.0), axis=1 - axis, keepdims=True)
    end = jnp.min(jnp.where(before, 4.0 * total, ends), axis=1 - axis, keepdims=True)
    first = jnp.floor(start * (1.0 / CHIP))
    last = jnp.floor((end - 1.0) * (1.0 / CHIP))
    owner = jnp.minimum(first + 1.0, last)
    inside = (place >= 0.0) & (place < total)
    return start, jnp.where(inside, owner, -9.0)


def kernel(
    n,
    len_hbm,
    q_hbm,
    k_hbm,
    v_hbm,
    g_hbm,
    o_ref,
    dq_ref,
    dk_ref,
    dv_ref,
    loaded,
    len_ref,
    own,
    stage,
    res_own,
    res_nb,
    send_r,
    send_l,
    recv_l,
    recv_r,
    fin,
    fin_out,
    fin_in,
    id_row,
    id_col,
    home,
    guest,
    load_sem,
    sib_send,
    sib_recv,
    r_send,
    r_recv,
    l_send,
    l_recv,
    cross_send,
    cross_recv,
    fin_send,
    fin_recv,
):
    me = lax.axis_index("ctx")
    core = lax.rem(me, 2)
    chip = lax.div(me, 2)
    sibling = me + 1 - 2 * core
    right = lax.rem(me + 2, n)
    left = lax.rem(me + n - 2, n)
    across = (lax.rem(sibling + 2, n), lax.rem(sibling + n - 2, n))
    mine = pl.ds(pl.multiple_of(core * ROWS, ROWS), ROWS)
    theirs = pl.ds(pl.multiple_of((1 - core) * ROWS, ROWS), ROWS)

    loads = [
        pltpu.make_async_copy(src, loaded.at[i], load_sem.at[i]) for i, src in enumerate((q_hbm, k_hbm, v_hbm, g_hbm))
    ]
    len_load = pltpu.make_async_copy(len_hbm, len_ref, load_sem.at[4])
    for load in (*loads, len_load):
        load.start()

    barrier = pltpu.get_barrier_semaphore()
    for other in (sibling, right, left, *across):
        pl.semaphore_signal(barrier, inc=1, device_id={"ctx": other}, device_id_type=pl.DeviceIdType.MESH)

    def remote(src, dst, send_sem, recv_sem, target):
        return pltpu.make_async_remote_copy(
            src_ref=src,
            dst_ref=dst,
            send_sem=send_sem,
            recv_sem=recv_sem,
            device_id={"ctx": target},
            device_id_type=pl.DeviceIdType.MESH,
        )

    def exchange(h):
        return remote(stage.at[h], own.at[h, :, mine], sib_send.at[h], sib_recv.at[h], sibling)

    def whole_slot(s, src_r, src_l):
        return (
            remote(src_r, recv_l.at[s], r_send.at[s], r_recv.at[s], right),
            remote(src_l, recv_r.at[s], l_send.at[s], l_recv.at[s], left),
        )

    def halved_slot(s, extra, straight, crossed):
        return (
            remote(straight, recv_l.at[s, :, mine], r_send.at[s], r_recv.at[s], right),
            remote(straight, recv_r.at[s, :, mine], l_send.at[s], l_recv.at[s], left),
            remote(crossed, recv_l.at[s, :, mine], cross_send.at[0, extra], cross_recv.at[0, extra], across[0]),
            remote(crossed, recv_r.at[s, :, mine], cross_send.at[1, extra], cross_recv.at[1, extra], across[1]),
        )

    def early_slot(s):
        return halved_slot(s, s, own.at[s, :, mine], stage.at[s])

    def late_slot(s):
        h = s - LAG
        return halved_slot(s, s - HEADS + LAG, res_nb.at[h, :, mine], res_nb.at[h, :, theirs])

    def hand_back(h):
        return remote(fin_out.at[h], fin_in.at[h], fin_send.at[h], fin_recv.at[h], sibling)

    def hand_raw(h):
        return remote(res_own.at[h, :, theirs], fin_in.at[h], fin_send.at[h], fin_recv.at[h], sibling)

    def packed(pair, half):
        lanes = pl.ds(pl.multiple_of(pair * 2 * DH, 2 * DH), 2 * DH)
        q, k, v, g = [loaded[i, :, lanes] for i in range(4)]
        return join(q, g, half), join(k, v, half)

    def pack(pair, _):
        for half in range(2):
            h = 2 * pair + half
            a, b = packed((1 - core) * (HEADS // 2) + pair, half)
            stage[h, 0] = a
            stage[h, 1] = b
            a, b = packed(core * (HEADS // 2) + pair, half)
            own[h, 0, mine] = a
            own[h, 1, mine] = b
        return 0

    for load in loads:
        load.wait()
    ready = (LAG + 1) // 2
    for pair in range(ready):
        pack(pair, 0)
    pl.semaphore_wait(barrier, 5)
    for s in range(LAG):
        for copy in early_slot(s):
            copy.start()
    for h in range(2 * ready):
        exchange(h).start()

    def pack_rest(pair, _):
        pack(pair, 0)
        exchange(2 * pair).start()
        exchange(2 * pair + 1).start()
        return 0

    lax.fori_loop(ready, HEADS // 2, pack_rest, 0)

    len_load.wait()
    here = chip.astype(F32)
    total = float(n * ROWS)
    docs = len_ref.shape[1]
    over = lax.broadcasted_iota(jnp.int32, (docs, docs), 1)
    down = lax.broadcasted_iota(jnp.int32, (docs, docs), 0)
    lengths = jnp.broadcast_to(len_ref[...].astype(F32), (docs, docs))
    ends_col = jnp.sum(jnp.where(over <= down, lengths, 0.0), axis=1, keepdims=True)
    ends_row = jnp.sum(jnp.where(over == down, ends_col, 0.0), axis=0, keepdims=True)
    for axis, ends in ((1, ends_col), (0, ends_row)):
        start_o, owner_o = token_info(ends, here * CHIP, axis, total)
        start_l, owner_l = token_info(ends, (here - 1.0) * CHIP, axis, total)
        start_r, owner_r = token_info(ends, (here + 1.0) * CHIP, axis, total)
        id_own = jnp.where(owner_o == here, start_o, -1.0)
        id_nb = jnp.where(owner_l == here, start_l, jnp.where(owner_r == here, start_r, -2.0))
        if axis == 1:
            id_row[:, 0:CHIP] = id_own
            id_row[:, CHIP:] = id_nb
        else:
            id_col[0:CHIP] = jnp.broadcast_to(id_own, (CHIP, 128))
            id_col[CHIP:] = jnp.broadcast_to(id_nb, (CHIP, 128))
            home[...] = jnp.broadcast_to(owner_o - here, (CHIP, 128)).astype(BF16)
            came = jnp.where(owner_l == here, -1.0, jnp.where(owner_r == here, 1.0, 0.0))
            guest[...] = jnp.broadcast_to(came, (CHIP, 128)).astype(BF16)

    def attend(t):
        came = guest[...]
        zero = jnp.zeros((CHIP, 2 * DH), BF16)
        both = []
        for i in range(2):
            nb = jnp.where(came < 0, recv_l[t, i], jnp.where(came > 0, recv_r[t, i], zero))
            both.append(jnp.concatenate([own[t, i], nb], axis=0))
        a, b = both
        at = a.T
        bt = b.T
        none = jnp.zeros((DH, 2 * CHIP), BF16)
        qt = jnp.concatenate([at[:DH], none], axis=0)
        gt = jnp.concatenate([none, at[DH:]], axis=0)
        ids = jnp.concatenate([id_col[...]] * (2 * CHIP // 128), axis=1)
        scores = jnp.dot(b, qt, preferred_element_type=F32)
        scores = jnp.where(ids == id_row[...], scores, -jnp.inf)
        top = jnp.max(scores, axis=0, keepdims=True)
        grown = jnp.exp2((scores - top) * (LOG2E / 8.0))
        probs = grown * (1.0 / jnp.sum(grown, axis=0, keepdims=True))
        probs_low = probs.astype(BF16)
        out = jnp.dot(bt[DH:], probs_low, preferred_element_type=F32).astype(BF16).astype(F32)
        delta = jnp.sum(out * at[DH:].astype(F32), axis=0, keepdims=True)
        prob_grads = jnp.dot(b, gt, preferred_element_type=F32)
        score_grads = (probs * (prob_grads - delta)).astype(BF16)
        dq = jnp.dot(bt[:DH], score_grads, preferred_element_type=F32) * 0.125
        first = jnp.concatenate([dq, out], axis=0).T.astype(BF16)
        dk = jnp.dot(score_grads, a, preferred_element_type=F32) * 0.125
        dv = jnp.dot(probs_low, a, preferred_element_type=F32)
        second = jnp.where(low_lanes((2 * CHIP, 2 * DH)), dk, dv).astype(BF16)
        for i, result in enumerate((first, second)):
            res_own[t, i] = result[:CHIP]
            res_nb[t, i] = result[CHIP:]

    def settle(h, at, rows, mid, out):
        for i in range(2):
            out[h, i] = jnp.where(
                at > 0, recv_r[h + LAG, i, rows], jnp.where(at < 0, recv_l[h + LAG, i, rows], mid[i])
            )

    def step(t, _):
        @pl.when(t < LAG)
        def _():
            for copy in early_slot(t):
                copy.wait_recv()
            exchange(t).wait_recv()

        @pl.when(t >= LAG)
        def _():
            for copy in whole_slot(t, own.at[0], own.at[0]):
                copy.wait_recv()

        attend(t)
        s = t + LAG

        @pl.when(s < HEADS)
        def _():
            exchange(s).wait_recv()
            at = home[...]
            for i in range(2):
                send_r[t, i] = jnp.where(at > 0, own[s, i], res_nb[t, i])
                send_l[t, i] = jnp.where(at < 0, own[s, i], res_nb[t, i])
            for copy in whole_slot(s, send_r.at[t], send_l.at[t]):
                copy.start()

        @pl.when(s >= HEADS)
        def _():
            for copy in late_slot(s):
                copy.start()
            hand_raw(t).start()

        @pl.when(t >= LAG)
        def _():
            h = t - LAG
            settle(h, home[theirs], theirs, res_own.at[h, :, theirs], fin_out)
            hand_back(h).start()
            settle(h, home[mine], mine, res_own.at[h, :, mine], fin)

        return 0

    lax.fori_loop(0, HEADS, step, 0)

    def unpack(source, pair, place):
        lanes = pl.ds(pl.multiple_of(place * 2 * DH, 2 * DH), 2 * DH)
        e, o = 2 * pair, 2 * pair + 1
        dq_ref[:, lanes] = join(source[e, 0], source[o, 0], 0)
        o_ref[:, lanes] = join(source[e, 0], source[o, 0], 1)
        dk_ref[:, lanes] = join(source[e, 1], source[o, 1], 0)
        dv_ref[:, lanes] = join(source[e, 1], source[o, 1], 1)

    def unpack_both(pair, _):
        unpack(fin, pair, core * (HEADS // 2) + pair)
        unpack(fin_in, pair, (1 - core) * (HEADS // 2) + pair)
        return 0

    def handed(h, _):
        hand_back(h).wait_recv()
        return 0

    lax.fori_loop(0, HEADS, handed, 0)
    settled = (HEADS - LAG) // 2
    lax.fori_loop(0, settled, unpack_both, 0)
    at = home[mine]
    for s in range(HEADS, SLOTS):
        h = s - LAG
        for copy in late_slot(s):
            copy.wait_recv()
        settle(h, at, mine, res_own.at[h, :, mine], fin)
        settle(h, at, theirs, fin_in.at[h], fin_in)
        if h % 2:
            unpack_both(h // 2, 0)

    def drain(h, _):
        exchange(h).wait_send()
        hand_back(h).wait_send()
        return 0

    def drain_slots(s, _):
        for copy in whole_slot(s, own.at[0], own.at[0]):
            copy.wait_send()
        return 0

    lax.fori_loop(0, HEADS, drain, 0)
    lax.fori_loop(LAG, HEADS, drain_slots, 0)
    for s in range(LAG):
        for copy in (*early_slot(s), *late_slot(HEADS + s)):
            copy.wait_send()


def write_out(*refs):
    sources, outs, sems = refs[:4], refs[4:8], refs[8]
    copies = [pltpu.make_async_copy(src, dst, sems.at[i]) for i, (src, dst) in enumerate(zip(sources, outs))]
    for copy in copies:
        copy.start()
    for copy in copies:
        copy.wait()


def on_device(queries, keys, values, cotangent, doc_lengths):
    n = lax.axis_size("ctx")
    block = (2, CHIP, 2 * DH)
    half = (2, ROWS, 2 * DH)
    vmem = pl.BlockSpec(memory_space=pltpu.VMEM)
    anywhere = pl.BlockSpec(memory_space=pl.ANY)
    pairs = 2 * CHIP * 2 * CHIP * HEADS
    outs = [jax.ShapeDtypeStruct(queries.shape, BF16)] * 4
    dma = pltpu.SemaphoreType.DMA
    queries, keys, values, cotangent, lengths = [
        pltpu.with_memory_space_constraint(x, pltpu.HBM)
        for x in (queries, keys, values, cotangent, doc_lengths.reshape(1, -1))
    ]
    results = pl.pallas_call(
        functools.partial(kernel, n),
        out_shape=[pltpu.VMEM(queries.shape, BF16)] * 4,
        in_specs=[anywhere] * 5,
        out_specs=[vmem] * 4,
        scratch_shapes=[
            pltpu.VMEM((4, *queries.shape), BF16),
            pltpu.VMEM((1, doc_lengths.shape[0]), jnp.int32),
            pltpu.VMEM((HEADS, *block), BF16),
            pltpu.VMEM((HEADS, *half), BF16),
            pltpu.VMEM((HEADS, *block), BF16),
            pltpu.VMEM((HEADS, *block), BF16),
            pltpu.VMEM((HEADS - LAG, *block), BF16),
            pltpu.VMEM((HEADS - LAG, *block), BF16),
            pltpu.VMEM((SLOTS, *block), BF16),
            pltpu.VMEM((SLOTS, *block), BF16),
            pltpu.VMEM((HEADS, *half), BF16),
            pltpu.VMEM((HEADS, *half), BF16),
            pltpu.VMEM((HEADS, *half), BF16),
            pltpu.VMEM((1, 2 * CHIP), F32),
            pltpu.VMEM((2 * CHIP, 128), F32),
            pltpu.VMEM((CHIP, 128), BF16),
            pltpu.VMEM((CHIP, 128), BF16),
            dma((5,)),
            dma((HEADS,)),
            dma((HEADS,)),
            dma((SLOTS,)),
            dma((SLOTS,)),
            dma((SLOTS,)),
            dma((SLOTS,)),
            dma((2, 2 * LAG)),
            dma((2, 2 * LAG)),
            dma((HEADS,)),
            dma((HEADS,)),
        ],
        compiler_params=pltpu.CompilerParams(
            collective_id=0, has_side_effects=True, vmem_limit_bytes=VMEM_LIMIT
        ),
        cost_estimate=pl.CostEstimate(flops=12 * DH * pairs, bytes_accessed=1 << 21, transcendentals=pairs),
    )(lengths, queries, keys, values, cotangent)
    return tuple(
        pl.pallas_call(
            write_out,
            out_shape=outs,
            in_specs=[vmem] * 4,
            out_specs=[anywhere] * 4,
            scratch_shapes=[dma((4,))],
            compiler_params=pltpu.CompilerParams(vmem_limit_bytes=16 * 1024 * 1024),
        )(*results)
    )


def solution(mesh):
    rows = P(("dp", "ctx"), None)
    return jax.shard_map(
        on_device,
        mesh=mesh,
        in_specs=(rows, rows, rows, rows, P("dp")),
        out_specs=(rows, rows, rows, rows),
        check_vma=False,
    )
```

time: 63 us -> 48 us (0.76)
  Pallas kernels: 54.9 us -> 47.3 us
  local copies, waits for them, and re-layouts: 7.26 us -> 0 us
    pallas_call x1 -> x2, Pallas kernels: 54.9 us -> 47.3 us  [the longest x1 46.3 us: on_device(): pl.pallas_call(functools.partial(kernel, n), out_shape=[pltpu.VMEM(querie...]
    unnamed x14 -> x0, local copies, waits for them, and re-layouts: 7.26 us -> none
where the time goes in v2:
time: 48 us; the launch traced here: 47.9 us
  Pallas kernels  47.3 us (99%)
  between operations  0.64 us (1%)
    pallas_call x1, Pallas kernels, on_device(): pl.pallas_call(functools.partial(kernel, n), out_shape=[pltpu.VMEM(querie...  46.3 us
    pallas_call x1, Pallas kernels, on_device(): pl.pallas_call(write_out, out_shape=outs, in_specs=[vmem] * 4, out_specs=...  1 us

profile of v2, /device:TPU:1, one launch (start us, length us, event | category | flops | bytes accessed | tf_op | source)
XLA Modules:
  0.0 47.9 jit_solution(7354665684856252191)
XLA Ops:
  0.6 46.3 %shard_map.84 = (bf16[128,1024]{1,0:T(8,128)(2,1)S(1)}, bf16[128,1024]{1,0:T(8,128)(2,1)S(1)}, bf16[128,1024]{1,0:T(8,128)(2,1)S(1)}, bf16[128,1024]{1,0:T(8,128)(2,1)S(1)}) custom-call(s32[1,64]{1,0:T(1,128)} %bitcast.1, bf16[128,1024]{1,0:T(8,128)(2,1)} %q_hbm.1, bf16[128,1024]{1,0:T(8,128)(2,1)} %k_hbm.1, bf16[128,1024]{1,0:T(8,128)(2,1)} %v_hbm.1, ...), custom_call_target="tpu_custom_call" | custom-call | flops 1610612736 | bytes 2097152 | tf_op jit(solution)/shard_map/pallas_call | solution.py:357
  46.9 1.0 %shard_map.85 = (bf16[128,1024]{1,0:T(8,128)(2,1)}, bf16[128,1024]{1,0:T(8,128)(2,1)}, bf16[128,1024]{1,0:T(8,128)(2,1)}, bf16[128,1024]{1,0:T(8,128)(2,1)}) custom-call(bf16[128,1024]{1,0:T(8,128)(2,1)S(1)} %get-tuple-element.8.refs_0_, bf16[128,1024]{1,0:T(8,128)(2,1)S(1)} %get-tuple-element.9.refs_1_, bf16[128,1024]{1,0:T(8,128)(2,1)S(1)} %get-tuple-element.10.refs_2_, ...), custom_call_target="tpu_custom_call" | custom-call | tf_op jit(solution)/shard_map/pallas_call | solution.py:398

commit v3 on v2

--- a/solution.py
+++ b/solution.py
@@ -99,9 +99,17 @@
     for load in (*loads, len_load):
         load.start()
 
+    has_left = chip > 0
+    has_right = chip < n // 2 - 1
     barrier = pltpu.get_barrier_semaphore()
-    for other in (sibling, right, left, *across):
-        pl.semaphore_signal(barrier, inc=1, device_id={"ctx": other}, device_id_type=pl.DeviceIdType.MESH)
+
+    def greet(others):
+        for other in others:
+            pl.semaphore_signal(barrier, inc=1, device_id={"ctx": other}, device_id_type=pl.DeviceIdType.MESH)
+
+    greet((sibling,))
+    pl.when(has_right)(lambda: greet((right, across[0])))
+    pl.when(has_left)(lambda: greet((left, across[1])))
 
     def remote(src, dst, send_sem, recv_sem, target):
         return pltpu.make_async_remote_copy(
@@ -118,17 +126,33 @@
 
     def whole_slot(s, src_r, src_l):
         return (
-            remote(src_r, recv_l.at[s], r_send.at[s], r_recv.at[s], right),
-            remote(src_l, recv_r.at[s], l_send.at[s], l_recv.at[s], left),
+            (remote(src_r, recv_l.at[s], r_send.at[s], r_recv.at[s], right),),
+            (remote(src_l, recv_r.at[s], l_send.at[s], l_recv.at[s], left),),
         )
 
     def halved_slot(s, extra, straight, crossed):
         return (
-            remote(straight, recv_l.at[s, :, mine], r_send.at[s], r_recv.at[s], right),
-            remote(straight, recv_r.at[s, :, mine], l_send.at[s], l_recv.at[s], left),
-            remote(crossed, recv_l.at[s, :, mine], cross_send.at[0, extra], cross_recv.at[0, extra], across[0]),
-            remote(crossed, recv_r.at[s, :, mine], cross_send.at[1, extra], cross_recv.at[1, extra], across[1]),
+            (
+                remote(straight, recv_l.at[s, :, mine], r_send.at[s], r_recv.at[s], right),
+                remote(crossed, recv_l.at[s, :, mine], cross_send.at[0, extra], cross_recv.at[0, extra], across[0]),
+            ),
+            (
+                remote(straight, recv_r.at[s, :, mine], l_send.at[s], l_recv.at[s], left),
+                remote(crossed, recv_r.at[s, :, mine], cross_send.at[1, extra], cross_recv.at[1, extra], across[1]),
+            ),
         )
+
+    def launch(slot):
+        pl.when(has_right)(lambda: [copy.start() for copy in slot[0]] and None)
+        pl.when(has_left)(lambda: [copy.start() for copy in slot[1]] and None)
+
+    def sent(slot):
+        pl.when(has_right)(lambda: [copy.wait_send() for copy in slot[0]] and None)
+        pl.when(has_left)(lambda: [copy.wait_send() for copy in slot[1]] and None)
+
+    def arrived(slot):
+        pl.when(has_left)(lambda: [copy.wait_recv() for copy in slot[0]] and None)
+        pl.when(has_right)(lambda: [copy.wait_recv() for copy in slot[1]] and None)
 
     def early_slot(s):
         return halved_slot(s, s, own.at[s, :, mine], stage.at[s])
@@ -164,10 +188,9 @@
     ready = (LAG + 1) // 2
     for pair in range(ready):
         pack(pair, 0)
-    pl.semaphore_wait(barrier, 5)
+    pl.semaphore_wait(barrier, 1 + 2 * has_left.astype(jnp.int32) + 2 * has_right.astype(jnp.int32))
     for s in range(LAG):
-        for copy in early_slot(s):
-            copy.start()
+        launch(early_slot(s))
     for h in range(2 * ready):
         exchange(h).start()
 
@@ -246,14 +269,12 @@
     def step(t, _):
         @pl.when(t < LAG)
         def _():
-            for copy in early_slot(t):
-                copy.wait_recv()
+            arrived(early_slot(t))
             exchange(t).wait_recv()
 
         @pl.when(t >= LAG)
         def _():
-            for copy in whole_slot(t, own.at[0], own.at[0]):
-                copy.wait_recv()
+            arrived(whole_slot(t, own.at[0], own.at[0]))
 
         attend(t)
         s = t + LAG
@@ -265,13 +286,11 @@
             for i in range(2):
                 send_r[t, i] = jnp.where(at > 0, own[s, i], res_nb[t, i])
                 send_l[t, i] = jnp.where(at < 0, own[s, i], res_nb[t, i])
-            for copy in whole_slot(s, send_r.at[t], send_l.at[t]):
-                copy.start()
+            launch(whole_slot(s, send_r.at[t], send_l.at[t]))
 
         @pl.when(s >= HEADS)
         def _():
-            for copy in late_slot(s):
-                copy.start()
+            launch(late_slot(s))
             hand_raw(t).start()
 
         @pl.when(t >= LAG)
@@ -308,8 +327,7 @@
     at = home[mine]
     for s in range(HEADS, SLOTS):
         h = s - LAG
-        for copy in late_slot(s):
-            copy.wait_recv()
+        arrived(late_slot(s))
         settle(h, at, mine, res_own.at[h, :, mine], fin)
         settle(h, at, theirs, fin_in.at[h], fin_in)
         if h % 2:
@@ -321,15 +339,14 @@
         return 0
 
     def drain_slots(s, _):
-        for copy in whole_slot(s, own.at[0], own.at[0]):
-            copy.wait_send()
+        sent(whole_slot(s, own.at[0], own.at[0]))
         return 0
 
     lax.fori_loop(0, HEADS, drain, 0)
     lax.fori_loop(LAG, HEADS, drain_slots, 0)
     for s in range(LAG):
-        for copy in (*early_slot(s), *late_slot(HEADS + s)):
-            copy.wait_send()
+        sent(early_slot(s))
+        sent(late_slot(HEADS + s))
 
 
 def write_out(*refs):

time: 48 us -> 46.4 us (0.967)
  the two profiles are of different devices: /device:TPU:1 before, /device:TPU:24 now
where the time goes in v3:
time: 46.4 us; the launch traced here: 45.7 us
  Pallas kernels  45 us (97%)
  between operations  0.64 us (1%)
    pallas_call x1, Pallas kernels, on_device(): pl.pallas_call(functools.partial(kernel, n), out_shape=[pltpu.VMEM(querie...  44 us
    pallas_call x1, Pallas kernels, on_device(): pl.pallas_call(write_out, out_shape=outs, in_specs=[vmem] * 4, out_specs=...  1 us

profile of v3, /device:TPU:24, one launch (start us, length us, event | category | flops | bytes accessed | tf_op | source)
XLA Modules:
  0.0 45.7 jit_solution(17881666746632694745)
XLA Ops:
  0.6 44.0 %shard_map.84 = (bf16[128,1024]{1,0:T(8,128)(2,1)S(1)}, bf16[128,1024]{1,0:T(8,128)(2,1)S(1)}, bf16[128,1024]{1,0:T(8,128)(2,1)S(1)}, bf16[128,1024]{1,0:T(8,128)(2,1)S(1)}) custom-call(s32[1,64]{1,0:T(1,128)} %bitcast.1, bf16[128,1024]{1,0:T(8,128)(2,1)} %q_hbm.1, bf16[128,1024]{1,0:T(8,128)(2,1)} %k_hbm.1, bf16[128,1024]{1,0:T(8,128)(2,1)} %v_hbm.1, ...), custom_call_target="tpu_custom_call" | custom-call | flops 1610612736 | bytes 2097152 | tf_op jit(solution)/shard_map/pallas_call | solution.py:374
  44.7 1.0 %shard_map.85 = (bf16[128,1024]{1,0:T(8,128)(2,1)}, bf16[128,1024]{1,0:T(8,128)(2,1)}, bf16[128,1024]{1,0:T(8,128)(2,1)}, bf16[128,1024]{1,0:T(8,128)(2,1)}) custom-call(bf16[128,1024]{1,0:T(8,128)(2,1)S(1)} %get-tuple-element.8.refs_0_, bf16[128,1024]{1,0:T(8,128)(2,1)S(1)} %get-tuple-element.9.refs_1_, bf16[128,1024]{1,0:T(8,128)(2,1)S(1)} %get-tuple-element.10.refs_2_, ...), custom_call_target="tpu_custom_call" | custom-call | tf_op jit(solution)/shard_map/pallas_call | solution.py:415

commit v4 on v3

--- a/solution.py
+++ b/solution.py
@@ -92,24 +92,24 @@
     mine = pl.ds(pl.multiple_of(core * ROWS, ROWS), ROWS)
     theirs = pl.ds(pl.multiple_of((1 - core) * ROWS, ROWS), ROWS)
 
+    has_left = chip > 0
+    has_right = chip < n // 2 - 1
+    barrier = pltpu.get_barrier_semaphore()
+
+    def greet(others):
+        for other in others:
+            pl.semaphore_signal(barrier, inc=1, device_id={"ctx": other}, device_id_type=pl.DeviceIdType.MESH)
+
+    greet((sibling,))
+    pl.when(has_right)(lambda: greet((right, across[0])))
+    pl.when(has_left)(lambda: greet((left, across[1])))
+
     loads = [
         pltpu.make_async_copy(src, loaded.at[i], load_sem.at[i]) for i, src in enumerate((q_hbm, k_hbm, v_hbm, g_hbm))
     ]
     len_load = pltpu.make_async_copy(len_hbm, len_ref, load_sem.at[4])
     for load in (*loads, len_load):
         load.start()
-
-    has_left = chip > 0
-    has_right = chip < n // 2 - 1
-    barrier = pltpu.get_barrier_semaphore()
-
-    def greet(others):
-        for other in others:
-            pl.semaphore_signal(barrier, inc=1, device_id={"ctx": other}, device_id_type=pl.DeviceIdType.MESH)
-
-    greet((sibling,))
-    pl.when(has_right)(lambda: greet((right, across[0])))
-    pl.when(has_left)(lambda: greet((left, across[1])))
 
     def remote(src, dst, send_sem, recv_sem, target):
         return pltpu.make_async_remote_copy(
@@ -185,14 +185,16 @@
 
     for load in loads:
         load.wait()
-    ready = (LAG + 1) // 2
-    for pair in range(ready):
-        pack(pair, 0)
+    pack(0, 0)
     pl.semaphore_wait(barrier, 1 + 2 * has_left.astype(jnp.int32) + 2 * has_right.astype(jnp.int32))
-    for s in range(LAG):
-        launch(early_slot(s))
-    for h in range(2 * ready):
-        exchange(h).start()
+    launch(early_slot(0))
+    launch(early_slot(1))
+    exchange(0).start()
+    exchange(1).start()
+    pack(1, 0)
+    launch(early_slot(2))
+    exchange(2).start()
+    exchange(3).start()
 
     def pack_rest(pair, _):
         pack(pair, 0)
@@ -200,7 +202,7 @@
         exchange(2 * pair + 1).start()
         return 0
 
-    lax.fori_loop(ready, HEADS // 2, pack_rest, 0)
+    lax.fori_loop(2, HEADS // 2, pack_rest, 0)
 
     len_load.wait()
     here = chip.astype(F32)
@@ -242,6 +244,7 @@
         gt = jnp.concatenate([none, at[DH:]], axis=0)
         ids = jnp.concatenate([id_col[...]] * (2 * CHIP // 128), axis=1)
         scores = jnp.dot(b, qt, preferred_element_type=F32)
+        prob_grads = jnp.dot(b, gt, preferred_element_type=F32)
         scores = jnp.where(ids == id_row[...], scores, -jnp.inf)
         top = jnp.max(scores, axis=0, keepdims=True)
         grown = jnp.exp2((scores - top) * (LOG2E / 8.0))
@@ -249,10 +252,9 @@
         probs_low = probs.astype(BF16)
         out = jnp.dot(bt[DH:], probs_low, preferred_element_type=F32).astype(BF16).astype(F32)
         delta = jnp.sum(out * at[DH:].astype(F32), axis=0, keepdims=True)
-        prob_grads = jnp.dot(b, gt, preferred_element_type=F32)
         score_grads = (probs * (prob_grads - delta)).astype(BF16)
         dq = jnp.dot(bt[:DH], score_grads, preferred_element_type=F32) * 0.125
-        first = jnp.concatenate([dq, out], axis=0).T.astype(BF16)
+        first = jnp.concatenate([dq, out], axis=0).astype(BF16).T
         dk = jnp.dot(score_grads, a, preferred_element_type=F32) * 0.125
         dv = jnp.dot(probs_low, a, preferred_element_type=F32)
         second = jnp.where(low_lanes((2 * CHIP, 2 * DH)), dk, dv).astype(BF16)

time: 46.4 us -> 46.4 us (level)
  no operation moved by 1% of the time
where the time goes in v4:
time: 46.4 us; the launch traced here: 45.7 us
  Pallas kernels  45.1 us (97%)
  between operations  0.64 us (1%)
    pallas_call x1, Pallas kernels, on_device(): pl.pallas_call(functools.partial(kernel, n), out_shape=[pltpu.VMEM(querie...  44.1 us
    pallas_call x1, Pallas kernels, on_device(): pl.pallas_call(write_out, out_shape=outs, in_specs=[vmem] * 4, out_specs=...  1 us

profile of v4, /device:TPU:24, one launch (start us, length us, event | category | flops | bytes accessed | tf_op | source)
XLA Modules:
  0.0 45.7 jit_solution(2450659310515773129)
XLA Ops:
  0.6 44.1 %shard_map.84 = (bf16[128,1024]{1,0:T(8,128)(2,1)S(1)}, bf16[128,1024]{1,0:T(8,128)(2,1)S(1)}, bf16[128,1024]{1,0:T(8,128)(2,1)S(1)}, bf16[128,1024]{1,0:T(8,128)(2,1)S(1)}) custom-call(s32[1,64]{1,0:T(1,128)} %bitcast.1, bf16[128,1024]{1,0:T(8,128)(2,1)} %q_hbm.1, bf16[128,1024]{1,0:T(8,128)(2,1)} %k_hbm.1, bf16[128,1024]{1,0:T(8,128)(2,1)} %v_hbm.1, ...), custom_call_target="tpu_custom_call" | custom-call | flops 1610612736 | bytes 2097152 | tf_op jit(solution)/shard_map/pallas_call | solution.py:376
  44.7 1.0 %shard_map.85 = (bf16[128,1024]{1,0:T(8,128)(2,1)}, bf16[128,1024]{1,0:T(8,128)(2,1)}, bf16[128,1024]{1,0:T(8,128)(2,1)}, bf16[128,1024]{1,0:T(8,128)(2,1)}) custom-call(bf16[128,1024]{1,0:T(8,128)(2,1)S(1)} %get-tuple-element.8.refs_0_, bf16[128,1024]{1,0:T(8,128)(2,1)S(1)} %get-tuple-element.9.refs_1_, bf16[128,1024]{1,0:T(8,128)(2,1)S(1)} %get-tuple-element.10.refs_2_, ...), custom_call_target="tpu_custom_call" | custom-call | tf_op jit(solution)/shard_map/pallas_call | solution.py:417

commit v5 on v4

--- a/solution.py
+++ b/solution.py
@@ -229,26 +229,57 @@
             came = jnp.where(owner_l == here, -1.0, jnp.where(owner_r == here, 1.0, 0.0))
             guest[...] = jnp.broadcast_to(came, (CHIP, 128)).astype(BF16)
 
-    def attend(t):
+    def turned(a, b):
+        at, bt = a.T, b.T
+        none = jnp.zeros((DH, CHIP), BF16)
+        return at, bt, jnp.concatenate([at[:DH], none], axis=0), jnp.concatenate([none, at[DH:]], axis=0)
+
+    def masked(b, qt, keys, queries):
+        ids = jnp.concatenate([id_col[keys]] * 2, axis=1)
+        return jnp.where(ids == id_row[:, queries], jnp.dot(b, qt, preferred_element_type=F32), -jnp.inf)
+
+    ours, nbs = slice(0, CHIP), slice(CHIP, 2 * CHIP)
+    rate = LOG2E / 8.0
+
+    def prepare(t):
+        a, b = own[t, 0], own[t, 1]
+        at, bt, qt, gt = turned(a, b)
+        scores = masked(b, qt, ours, ours)
+        top = jnp.max(scores, axis=0, keepdims=True)
+        grown = jnp.exp2((scores - top) * rate)
+        total = jnp.sum(grown, axis=0, keepdims=True)
+        return a, b, at, bt, qt, gt, top, grown, total, jnp.dot(b, gt, preferred_element_type=F32)
+
+    def attend(t, prepared):
+        a_o, b_o, at_o, bt_o, qt_o, gt_o, top_o, grown_o, total_o, prob_grads_o = prepared
         came = guest[...]
         zero = jnp.zeros((CHIP, 2 * DH), BF16)
-        both = []
-        for i in range(2):
-            nb = jnp.where(came < 0, recv_l[t, i], jnp.where(came > 0, recv_r[t, i], zero))
-            both.append(jnp.concatenate([own[t, i], nb], axis=0))
-        a, b = both
-        at = a.T
-        bt = b.T
-        none = jnp.zeros((DH, 2 * CHIP), BF16)
-        qt = jnp.concatenate([at[:DH], none], axis=0)
-        gt = jnp.concatenate([none, at[DH:]], axis=0)
-        ids = jnp.concatenate([id_col[...]] * (2 * CHIP // 128), axis=1)
-        scores = jnp.dot(b, qt, preferred_element_type=F32)
-        prob_grads = jnp.dot(b, gt, preferred_element_type=F32)
-        scores = jnp.where(ids == id_row[...], scores, -jnp.inf)
-        top = jnp.max(scores, axis=0, keepdims=True)
-        grown = jnp.exp2((scores - top) * (LOG2E / 8.0))
-        probs = grown * (1.0 / jnp.sum(grown, axis=0, keepdims=True))
+        a_n, b_n = [
+            jnp.where(came < 0, recv_l[t, i], jnp.where(came > 0, recv_r[t, i], zero)) for i in range(2)
+        ]
+        at_n, bt_n, qt_n, gt_n = turned(a_n, b_n)
+        a = jnp.concatenate([a_o, a_n], axis=0)
+        b = jnp.concatenate([b_o, b_n], axis=0)
+        at = jnp.concatenate([at_o, at_n], axis=1)
+        bt = jnp.concatenate([bt_o, bt_n], axis=1)
+        scores = masked(b_n, qt_o, nbs, ours)
+        scores_n = masked(b, qt_n, slice(0, 2 * CHIP), nbs)
+        prob_grads = jnp.concatenate(
+            [
+                jnp.concatenate([prob_grads_o, jnp.dot(b_n, gt_o, preferred_element_type=F32)], axis=0),
+                jnp.dot(b, gt_n, preferred_element_type=F32),
+            ],
+            axis=1,
+        )
+        top = jnp.maximum(top_o, jnp.max(scores, axis=0, keepdims=True))
+        grown = jnp.exp2((scores - top) * rate)
+        shrink = jnp.exp2((top_o - top) * rate)
+        share = 1.0 / (total_o * shrink + jnp.sum(grown, axis=0, keepdims=True))
+        probs_o = jnp.concatenate([grown_o * (shrink * share), grown * share], axis=0)
+        top_n = jnp.max(scores_n, axis=0, keepdims=True)
+        grown_n = jnp.exp2((scores_n - top_n) * rate)
+        probs_n = grown_n * (1.0 / jnp.sum(grown_n, axis=0, keepdims=True))
+        probs = jnp.concatenate([probs_o, probs_n], axis=1)
         probs_low = probs.astype(BF16)
         out = jnp.dot(bt[DH:], probs_low, preferred_element_type=F32).astype(BF16).astype(F32)
         delta = jnp.sum(out * at[DH:].astype(F32), axis=0, keepdims=True)
@@ -271,14 +302,19 @@
     def step(t, _):
         @pl.when(t < LAG)
         def _():
+            exchange(t).wait_recv()
+
+        prepared = prepare(t)
+
+        @pl.when(t < LAG)
+        def _():
             arrived(early_slot(t))
-            exchange(t).wait_recv()
 
         @pl.when(t >= LAG)
         def _():
             arrived(whole_slot(t, own.at[0], own.at[0]))
 
-        attend(t)
+        attend(t, prepared)
         s = t + LAG
 
         @pl.when(s < HEADS)

time: 46.4 us -> 46.3 us (level)
  no operation moved by 1% of the time
where the time goes in v5:
time: 46.3 us; the launch traced here: 45.5 us
  Pallas kernels  44.9 us (97%)
  between operations  0.64 us (1%)
    pallas_call x1, Pallas kernels, on_device(): pl.pallas_call(functools.partial(kernel, n), out_shape=[pltpu.VMEM(querie...  43.9 us
    pallas_call x1, Pallas kernels, on_device(): pl.pallas_call(write_out, out_shape=outs, in_specs=[vmem] * 4, out_specs=...  1 us

profile of v5, /device:TPU:24, one launch (start us, length us, event | category | flops | bytes accessed | tf_op | source)
XLA Modules:
  0.0 45.5 jit_solution(569531549395199669)
XLA Ops:
  0.6 43.9 %shard_map.84 = (bf16[128,1024]{1,0:T(8,128)(2,1)S(1)}, bf16[128,1024]{1,0:T(8,128)(2,1)S(1)}, bf16[128,1024]{1,0:T(8,128)(2,1)S(1)}, bf16[128,1024]{1,0:T(8,128)(2,1)S(1)}) custom-call(s32[1,64]{1,0:T(1,128)} %bitcast.1, bf16[128,1024]{1,0:T(8,128)(2,1)} %q_hbm.1, bf16[128,1024]{1,0:T(8,128)(2,1)} %k_hbm.1, bf16[128,1024]{1,0:T(8,128)(2,1)} %v_hbm.1, ...), custom_call_target="tpu_custom_call" | custom-call | flops 1610612736 | bytes 2097152 | tf_op jit(solution)/shard_map/pallas_call | solution.py:412
  44.5 1.0 %shard_map.85 = (bf16[128,1024]{1,0:T(8,128)(2,1)}, bf16[128,1024]{1,0:T(8,128)(2,1)}, bf16[128,1024]{1,0:T(8,128)(2,1)}, bf16[128,1024]{1,0:T(8,128)(2,1)}) custom-call(bf16[128,1024]{1,0:T(8,128)(2,1)S(1)} %get-tuple-element.8.refs_0_, bf16[128,1024]{1,0:T(8,128)(2,1)S(1)} %get-tuple-element.9.refs_1_, bf16[128,1024]{1,0:T(8,128)(2,1)S(1)} %get-tuple-element.10.refs_2_, ...), custom_call_target="tpu_custom_call" | custom-call | tf_op jit(solution)/shard_map/pallas_call | solution.py:453

commit v6 on v4

--- a/solution.py
+++ b/solution.py
@@ -143,8 +143,10 @@
         )
 
     def launch(slot):
-        pl.when(has_right)(lambda: [copy.start() for copy in slot[0]] and None)
-        pl.when(has_left)(lambda: [copy.start() for copy in slot[1]] and None)
+        if slot[0]:
+            pl.when(has_right)(lambda: [copy.start() for copy in slot[0]] and None)
+        if slot[1]:
+            pl.when(has_left)(lambda: [copy.start() for copy in slot[1]] and None)
 
     def sent(slot):
         pl.when(has_right)(lambda: [copy.wait_send() for copy in slot[0]] and None)
@@ -285,10 +287,13 @@
         def _():
             exchange(s).wait_recv()
             at = home[...]
+            to_right, to_left = whole_slot(s, send_r.at[t], send_l.at[t])
             for i in range(2):
                 send_r[t, i] = jnp.where(at > 0, own[s, i], res_nb[t, i])
+            launch((to_right, ()))
+            for i in range(2):
                 send_l[t, i] = jnp.where(at < 0, own[s, i], res_nb[t, i])
-            launch(whole_slot(s, send_r.at[t], send_l.at[t]))
+            launch(((), to_left))
 
         @pl.when(s >= HEADS)
         def _():

time: 46.4 us -> 46.4 us (level)
  no operation moved by 1% of the time
where the time goes in v6:
time: 46.4 us; the launch traced here: 45.7 us
  Pallas kernels  45 us (97%)
  between operations  0.64 us (1%)
    pallas_call x1, Pallas kernels, on_device(): pl.pallas_call(functools.partial(kernel, n), out_shape=[pltpu.VMEM(querie...  44 us
    pallas_call x1, Pallas kernels, on_device(): pl.pallas_call(write_out, out_shape=outs, in_specs=[vmem] * 4, out_specs=...  1 us

profile of v6, /device:TPU:24, one launch (start us, length us, event | category | flops | bytes accessed | tf_op | source)
XLA Modules:
  0.0 45.7 jit_solution(8382467968166609624)
XLA Ops:
  0.6 44.0 %shard_map.84 = (bf16[128,1024]{1,0:T(8,128)(2,1)S(1)}, bf16[128,1024]{1,0:T(8,128)(2,1)S(1)}, bf16[128,1024]{1,0:T(8,128)(2,1)S(1)}, bf16[128,1024]{1,0:T(8,128)(2,1)S(1)}) custom-call(s32[1,64]{1,0:T(1,128)} %bitcast.1, bf16[128,1024]{1,0:T(8,128)(2,1)} %q_hbm.1, bf16[128,1024]{1,0:T(8,128)(2,1)} %k_hbm.1, bf16[128,1024]{1,0:T(8,128)(2,1)} %v_hbm.1, ...), custom_call_target="tpu_custom_call" | custom-call | flops 1610612736 | bytes 2097152 | tf_op jit(solution)/shard_map/pallas_call | solution.py:381
  44.7 1.0 %shard_map.85 = (bf16[128,1024]{1,0:T(8,128)(2,1)}, bf16[128,1024]{1,0:T(8,128)(2,1)}, bf16[128,1024]{1,0:T(8,128)(2,1)}, bf16[128,1024]{1,0:T(8,128)(2,1)}) custom-call(bf16[128,1024]{1,0:T(8,128)(2,1)S(1)} %get-tuple-element.8.refs_0_, bf16[128,1024]{1,0:T(8,128)(2,1)S(1)} %get-tuple-element.9.refs_1_, bf16[128,1024]{1,0:T(8,128)(2,1)S(1)} %get-tuple-element.10.refs_2_, ...), custom_call_target="tpu_custom_call" | custom-call | tf_op jit(solution)/shard_map/pallas_call | solution.py:422

commit v7 on v6

--- a/solution.py
+++ b/solution.py
@@ -305,7 +305,6 @@
             h = t - LAG
             settle(h, home[theirs], theirs, res_own.at[h, :, theirs], fin_out)
             hand_back(h).start()
-            settle(h, home[mine], mine, res_own.at[h, :, mine], fin)
 
         return 0
 
@@ -328,6 +327,11 @@
         hand_back(h).wait_recv()
         return 0
 
+    def settle_mine(h, _):
+        settle(h, home[mine], mine, res_own.at[h, :, mine], fin)
+        return 0
+
+    lax.fori_loop(0, HEADS - LAG, settle_mine, 0)
     lax.fori_loop(0, HEADS, handed, 0)
     settled = (HEADS - LAG) // 2
     lax.fori_loop(0, settled, unpack_both, 0)

time: 46.4 us -> 46.4 us (level)
  no operation moved by 1% of the time
where the time goes in v7:
time: 46.4 us; the launch traced here: 45.7 us
  Pallas kernels  45 us (97%)
  between operations  0.64 us (1%)
    pallas_call x1, Pallas kernels, on_device(): pl.pallas_call(functools.partial(kernel, n), out_shape=[pltpu.VMEM(querie...  44 us
    pallas_call x1, Pallas kernels, on_device(): pl.pallas_call(write_out, out_shape=outs, in_specs=[vmem] * 4, out_specs=...  1 us

profile of v7, /device:TPU:24, one launch (start us, length us, event | category | flops | bytes accessed | tf_op | source)
XLA Modules:
  0.0 45.7 jit_solution(8276994358679499577)
XLA Ops:
  0.6 44.0 %shard_map.84 = (bf16[128,1024]{1,0:T(8,128)(2,1)S(1)}, bf16[128,1024]{1,0:T(8,128)(2,1)S(1)}, bf16[128,1024]{1,0:T(8,128)(2,1)S(1)}, bf16[128,1024]{1,0:T(8,128)(2,1)S(1)}) custom-call(s32[1,64]{1,0:T(1,128)} %bitcast.1, bf16[128,1024]{1,0:T(8,128)(2,1)} %q_hbm.1, bf16[128,1024]{1,0:T(8,128)(2,1)} %k_hbm.1, bf16[128,1024]{1,0:T(8,128)(2,1)} %v_hbm.1, ...), custom_call_target="tpu_custom_call" | custom-call | flops 1610612736 | bytes 2097152 | tf_op jit(solution)/shard_map/pallas_call | solution.py:385
  44.7 1.0 %shard_map.85 = (bf16[128,1024]{1,0:T(8,128)(2,1)}, bf16[128,1024]{1,0:T(8,128)(2,1)}, bf16[128,1024]{1,0:T(8,128)(2,1)}, bf16[128,1024]{1,0:T(8,128)(2,1)}) custom-call(bf16[128,1024]{1,0:T(8,128)(2,1)S(1)} %get-tuple-element.8.refs_0_, bf16[128,1024]{1,0:T(8,128)(2,1)S(1)} %get-tuple-element.9.refs_1_, bf16[128,1024]{1,0:T(8,128)(2,1)S(1)} %get-tuple-element.10.refs_2_, ...), custom_call_target="tpu_custom_call" | custom-call | tf_op jit(solution)/shard_map/pallas_call | solution.py:426
